TPU v7x, 512 devices: a whole 4x8x8 slice. The times are simulated.
512 devices in a mesh: slab: 128 (over z, y_hi, x), cross: 4 (over y_lo, core).
Axes of the slice: x: 4, y: 8 (y_hi: 4, y_lo: 2; y = y_hi * 2 + y_lo), z: 8, core: 2. Of those that a mesh axis runs over, the one named last changes fastest.
Arguments:
- features: bfloat16 [128, 4, 2, 96, 512], P('slab', 'cross'), may hold values from -6 to 6
- out_grad: bfloat16 [128, 4, 2, 192, 512], P('slab', 'cross'), may hold values from -6 to 6
- weights: bfloat16 [7, 96, 192], replicated, may hold values from -0.25 to 0.25
- conv_bias: float32 [192], replicated, may hold values from -1 to 1
- brick_count: int32 [128, 4], P('slab', 'cross'), may hold values from 2 to 2, as said below
- neighbours: int32 [128, 4, 2, 6], P('slab', 'cross'), may hold values from 3 to 20, as said below
- send_slab: int32 [128, 4, 2, 2], P('slab', 'cross'), may hold values from 0 to 12, as said below
- send_cross: int32 [128, 4, 2, 2], P('slab', 'cross'), may hold values from 2 to 12, as said below
Outputs:
- grad_features: bfloat16 [128, 4, 2, 96, 512], P('slab', 'cross')
- grad_weights: float32 [7, 96, 192], replicated
- grad_bias: float32 [192], replicated
Inputs may be any that keep to these rules, and one draw needn't show every extreme that they name: Live bricks fill the first brick_count slots of a device; some device has all 2 slots live. `neighbours`: directions f = 0..5 are -x, +x, -y, +y, -z, +z. An entry below 12 names row 6 c + (f xor 1) of a live brick c of the same device; entries from 12 to 19 name received faces, the received slots of a list being named in list order; 20 is the zero row. No row other than the zero row is named twice; empty slots name only the zero row. `send_slab`: each row lists 6 b + f of live bricks in increasing order (f = 1 in row 0, f = 0 in row 1), then the value 6 * 2; in some device a row lists 2 faces. `send_cross`: each row lists 6 b + f of live bricks in increasing order (f = 3 in row 0, f = 2 in row 1), then the value 6 * 2; in some device a row lists 2 faces.
All inputs are finite; a program needn't handle non-finite values.
Results may differ from a plain program's by a relative error of at most 0.0075.
Values may be sent and summed in bfloat16 or wider, within the bound.
No kernel may reach another device: no remote copies, remote signals or barrier semaphores. Data moves between devices by JAX's collectives and lax.ppermute only.
A program may use at most 64 MiB of HBM per device.

v0:
```python
from functools import partial
import math

import jax
import jax.numpy as jnp
from jax import lax
from jax.sharding import PartitionSpec as P

EDGE = 8


highest = lax.Precision.HIGHEST


def shifted(value, axis, steps):
    count = lax.axis_size(axis)
    initial, last = (max(0, -steps), min(count, count - steps))
    return lax.ppermute(value, axis, [(source, source + steps) for source in range(initial, last)])


def face_layers(bricks):
    number, channels = (bricks.shape[0], bricks.shape[1])
    boundary = [
        bricks[:, :, 0],
        bricks[:, :, -1],
        bricks[:, :, :, 0],
        bricks[:, :, :, -1],
        bricks[:, :, :, :, 0],
        bricks[:, :, :, :, -1],
    ]
    return jnp.stack([layer_face.reshape(number, channels, -1) for layer_face in boundary], axis=1)


def tap_field(tap_index, bricks, beside):
    if tap_index == 0:
        return bricks
    if tap_index == 1:
        return jnp.concatenate([beside[:, 0][:, :, None], bricks[:, :, :-1]], axis=2)
    if tap_index == 2:
        return jnp.concatenate([bricks[:, :, 1:], beside[:, 1][:, :, None]], axis=2)
    if tap_index == 3:
        return jnp.concatenate([beside[:, 2][:, :, :, None], bricks[:, :, :, :-1]], axis=3)
    if tap_index == 4:
        return jnp.concatenate([bricks[:, :, :, 1:], beside[:, 3][:, :, :, None]], axis=3)
    if tap_index == 5:
        return jnp.concatenate([beside[:, 4][..., None], bricks[..., :-1]], axis=4)
    return jnp.concatenate([bricks[..., 1:], beside[:, 5][..., None]], axis=4)


def spread_rows(values, indices, total_rows):
    selector = (indices[:, None] == jnp.arange(total_rows, dtype=jnp.int32)[None, :]).astype(
        jnp.float32
    )
    return jnp.einsum("mk,md->kd", selector, values, precision=highest)


def silu_slope(pre_act):
    sigmoid_pre = jax.nn.sigmoid(pre_act)
    return sigmoid_pre * (1.0 + pre_act * (1.0 - sigmoid_pre))


def shift_slab(payload, offset):
    return shifted(payload, "slab", offset)


def shift_cross(payload, offset):
    return shifted(payload, "cross", offset)


def return_slab(payload, offset):
    return shifted(payload.astype(jnp.bfloat16), "slab", offset).astype(payload.dtype)


def return_cross(payload, offset):
    return shifted(payload.astype(jnp.bfloat16), "cross", offset).astype(payload.dtype)


def local(features, out_grad, weights, conv_bias, brick_count, neighbours, send_slab, send_cross):
    inputs = features[0, 0]
    upstream = out_grad[0, 0]
    number, channels, voxels = inputs.shape
    edge_len = EDGE
    layer_size = edge_len * edge_len
    row_width = channels * layer_size
    link_rows = neighbours[0, 0].reshape(-1)
    slab_list = send_slab[0, 0]
    cross_list = send_cross[0, 0]
    slab_faces = slab_list.shape[1]
    cross_faces = cross_list.shape[1]
    local_rows = number * 6
    cubes = inputs.reshape(number, channels, edge_len, edge_len, edge_len)
    own_faces = face_layers(cubes).reshape(local_rows, row_width)
    zero_row = jnp.zeros((1, row_width), own_faces.dtype)
    padded = jnp.concatenate([own_faces, zero_row], axis=0)
    slab_sent = jnp.take(padded, slab_list, axis=0)
    cross_sent = jnp.take(padded, cross_list, axis=0)
    slab_low = shift_slab(slab_sent[0], 1)
    slab_high = shift_slab(slab_sent[1], -1)
    cross_low = shift_cross(cross_sent[0], 1)
    cross_high = shift_cross(cross_sent[1], -1)
    face_table = jnp.concatenate(
        [own_faces, slab_low, slab_high, cross_low, cross_high, zero_row], axis=0
    )
    table_rows = face_table.shape[0]
    beside = jnp.take(face_table, link_rows, axis=0).reshape(
        number, 6, channels, edge_len, edge_len
    )
    fields = [
        tap_field(tap_index, cubes, beside).reshape(number, channels, voxels)
        for tap_index in range(7)
    ]
    pre_act = conv_bias[None, :, None]
    for tap_index in range(7):
        pre_act = pre_act + jnp.einsum(
            "io,biv->bov", weights[tap_index], fields[tap_index], preferred_element_type=jnp.float32
        )
    live_slot = jnp.arange(number, dtype=jnp.int32) < brick_count[0, 0]
    grad_pre = jnp.where(live_slot[:, None, None], upstream * silu_slope(pre_act), 0.0).astype(
        jnp.bfloat16
    )
    weight_terms = jnp.stack(
        [
            jnp.einsum(
                "biv,bov->io", fields[tap_index], grad_pre, preferred_element_type=jnp.float32
            )
            for tap_index in range(7)
        ]
    )
    bias_terms = jnp.sum(grad_pre, axis=(0, 2), dtype=jnp.float32)
    summed_weights, summed_bias = lax.psum((weight_terms, bias_terms), ("slab", "cross"))
    zero_cube = jnp.zeros(cubes.shape, jnp.float32)
    zero_beside = jnp.zeros(beside.shape, jnp.float32)
    grad_cube = zero_cube
    grad_beside = zero_beside
    for tap_index in range(7):
        tap_grad = jnp.einsum(
            "io,bov->biv", weights[tap_index], grad_pre, preferred_element_type=jnp.float32
        ).reshape(cubes.shape)
        _, pullback = jax.vjp(partial(tap_field, tap_index), zero_cube, zero_beside)
        part_cube, part_beside = pullback(tap_grad)
        grad_cube = grad_cube + part_cube
        grad_beside = grad_beside + part_beside
    grad_table = spread_rows(grad_beside.reshape(local_rows, row_width), link_rows, table_rows)
    first_high = local_rows + slab_faces
    first_cross_low = first_high + slab_faces
    first_cross_high = first_cross_low + cross_faces
    last_row = first_cross_high + cross_faces
    returned_slab = jnp.concatenate(
        [
            return_slab(grad_table[local_rows:first_high], -1),
            return_slab(grad_table[first_high:first_cross_low], 1),
        ],
        axis=0,
    )
    returned_cross = jnp.concatenate(
        [
            return_cross(grad_table[first_cross_low:first_cross_high], -1),
            return_cross(grad_table[first_cross_high:last_row], 1),
        ],
        axis=0,
    )
    face_grad = grad_table[:local_rows]
    face_grad = (
        face_grad + spread_rows(returned_slab, slab_list.reshape(-1), local_rows + 1)[:local_rows]
    )
    face_grad = (
        face_grad + spread_rows(returned_cross, cross_list.reshape(-1), local_rows + 1)[:local_rows]
    )
    _, face_pull = jax.vjp(face_layers, zero_cube)
    grad_total = grad_cube + face_pull(face_grad.reshape(number, 6, channels, layer_size))[0]
    grad_features = grad_total.reshape(number, channels, voxels).astype(jnp.bfloat16)[None, None]
    norm_scale = 1.0 / math.sqrt(lax.axis_size("slab") * lax.axis_size("cross") * number * voxels)
    return (grad_features, summed_weights * norm_scale, summed_bias * norm_scale)


def solution(mesh):
    in_specs = (
        P("slab", "cross", None, None, None),
        P("slab", "cross", None, None, None),
        P(),
        P(),
        P("slab", "cross"),
        P("slab", "cross", None, None),
        P("slab", "cross", None, None),
        P("slab", "cross", None, None),
    )
    out_specs = (P("slab", "cross", None, None, None), P(), P())
    return jax.shard_map(local, mesh=mesh, in_specs=in_specs, out_specs=out_specs, check_vma=False)
```

profile of v0, /device:TPU:1, one launch (start us, length us, event | category | flops | bytes accessed | tf_op | source)
XLA Modules:
  0.0 469.4 jit_solution(12628964416548235628)
XLA Ops:
  8.6 1.1 copy.116
  12.0 1.3 collective-permute-start.1
  13.3 4.6 collective-permute-start
  19.4 8.8 %collective-permute-start.3 = (bf16[2,6144]{1,0:T(2,128)(2,1)S(1)}, bf16[2,6144]{1,0:T(2,128)(2,1)S(1)}, u32[]{:S(2)}, u32[]{:S(2)}) collective-permute-start(bf16[2,6144]{1,0:T(2,128)(2,1)S(1)} %get-tuple-element.37), channel_id=1, source_target_pairs={{1,0},{2,1},{3,2},{5,4},{6,5},{7,6},{9,8},{10,9},{11,10},{13,12},{... | collective-permute-start | bytes 73736 | tf_op jit(solution)/shard_map/ppermute | solution.py:18
  28.2 1.9 collective-permute-start.2
  33.1 0.9 fusion.73
  33.9 0.8 fusion.74
  39.0 2.9 gather.10
  41.8 1.2 copy.118
  44.4 1.0 pad_maximum_fusion.1
  46.8 0.8 convert_reduce_fusion
  47.7 1.0 convolution_bitcast_fusion.6
  49.0 1.0 convolution_bitcast_fusion.3
  50.0 1.0 convolution_bitcast_fusion.2
  51.0 1.0 convolution_bitcast_fusion.1
  51.9 0.9 convolution_bitcast_fusion
  52.9 0.9 fusion.14
  53.8 104.4 %psum.15 = f32[192]{0:T(256)S(1)} all-reduce(f32[192]{0:T(256)S(1)} %get-tuple-element.43), channel_id=1, replica_groups=mesh['slab'=128,'cross'=4] {'slab','cross'}, use_global_device_ids=true, to_apply=%region_2.4 | all-reduce | flops 192 | bytes 1536 | tf_op jit(solution)/shard_map/psum | solution.py:130
  159.9 1.2 copy.143
  161.8 2.0 copy.145
  163.8 1.5 slice_bitcast_fusion
  165.2 1.2 copy.147
  167.1 1.2 copy.149
  169.0 0.9 fusion.13
  169.9 0.9 fusion.12
  170.8 0.9 fusion.11
  171.7 0.9 fusion.10
  172.5 0.9 fusion.9
  173.4 0.9 fusion.8
  174.3 1.0 pad_add_fusion
  175.4 2.9 copy.155
  178.3 6.9 %reshape.148 = f32[12,6144]{1,0:T(8,128)} reshape(f32[2,6,96,8,8]{4,3,2,1,0:T(8,128)} %copy.155) | data formatting | bytes 589824 | tf_op jit(solution)/shard_map/reshape | solution.py:143
  185.2 2.4 fusion.77
  188.3 2.2 collective-permute-start.7
  190.4 2.8 collective-permute-start.6
  195.4 0.8 split.50
  197.3 1.3 collective-permute-start.4
  198.7 4.0 collective-permute-start.5
  202.7 1.0 fusion.22
  203.7 2.0 fusion
  205.8 1.2 reshape.149
  207.7 1.0 copy.156
  208.7 1.0 copy.163
  209.7 1.0 copy.162
  210.9 1.6 add_convert_fusion
  213.3 247.0 %all-reduce.21.cloned.1.call-done = f32[7,96,192]{1,2,0:T(8,128)} async-done(((f32[7,96,192]{1,2,0:T(8,128)}), f32[7,96,192]{1,2,0:T(8,128)}) %all-reduce.21.cloned.1.call-update) | async-done | bytes 516112 | tf_op jit(solution)/shard_map/psum | solution.py:130
  460.3 1.2 broadcast_multiply_fusion
  461.4 1.1 copy.177
  (130 shorter events, 24.0 us)
Async XLA Ops:
  7.2 30.1 %copy-start.19 = (s32[1,1,2,6]{3,2,1,0:T(2,128)S(1)}, s32[1,1,2,6]{3,2,1,0:T(2,128)}, u32[]{:S(2)}) copy-start(s32[1,1,2,6]{3,2,1,0:T(2,128)} %param.15) | copy-start | bytes 148
  7.2 453.1 %all-reduce.21.cloned.1.call-start = ((), (), s32[]{:S(2)}) async-start(), calls=%async_computation | async-start | bytes 1376256 | tf_op jit(solution)/shard_map/psum | solution.py:130
  12.0 25.9 %collective-permute-start.1 = (bf16[2,6144]{1,0:T(2,128)(2,1)S(1)}, bf16[2,6144]{1,0:T(2,128)(2,1)S(1)}, u32[]{:S(2)}, u32[]{:S(2)}) collective-permute-start(bf16[2,6144]{1,0:T(2,128)(2,1)S(1)} %get-tuple-element.39), channel_id=1, source_target_pairs={{4,0},{8,4},{12,8},{16,12},{20,16},{24,20},{28,24},{32,28},{36,32}... | collective-permute-start | bytes 73736 | tf_op jit(solution)/shard_map/ppermute | solution.py:18
  13.3 24.6 %collective-permute-start = (bf16[2,6144]{1,0:T(2,128)(2,1)S(1)}, bf16[2,6144]{1,0:T(2,128)(2,1)S(1)}, u32[]{:S(2)}, u32[]{:S(2)}) collective-permute-start(bf16[2,6144]{1,0:T(2,128)(2,1)S(1)} %get-tuple-element.40), channel_id=1, source_target_pairs={{0,4},{4,8},{8,12},{12,16},{16,20},{20,24},{24,28},{28,32},{32,36}... | collective-permute-start | bytes 73736 | tf_op jit(solution)/shard_map/ppermute | solution.py:18
  19.4 18.6 %collective-permute-start.3 = (bf16[2,6144]{1,0:T(2,128)(2,1)S(1)}, bf16[2,6144]{1,0:T(2,128)(2,1)S(1)}, u32[]{:S(2)}, u32[]{:S(2)}) collective-permute-start(bf16[2,6144]{1,0:T(2,128)(2,1)S(1)} %get-tuple-element.37), channel_id=1, source_target_pairs={{1,0},{2,1},{3,2},{5,4},{6,5},{7,6},{9,8},{10,9},{11,10},{13,12},{... | collective-permute-start | bytes 73736 | tf_op jit(solution)/shard_map/ppermute | solution.py:18
  28.2 9.8 %collective-permute-start.2 = (bf16[2,6144]{1,0:T(2,128)(2,1)S(1)}, bf16[2,6144]{1,0:T(2,128)(2,1)S(1)}, u32[]{:S(2)}, u32[]{:S(2)}) collective-permute-start(bf16[2,6144]{1,0:T(2,128)(2,1)S(1)} %get-tuple-element.38), channel_id=1, source_target_pairs={{0,1},{1,2},{2,3},{4,5},{5,6},{6,7},{8,9},{9,10},{10,11},{12,13},{... | collective-permute-start | bytes 73736 | tf_op jit(solution)/shard_map/ppermute | solution.py:18
  38.0 5.7 %copy-start.8 = (bf16[7,96,192]{2,1,0:T(8,128)(2,1)S(1)}, bf16[7,96,192]{2,1,0:T(8,128)(2,1)}, u32[]{:S(2)}) copy-start(bf16[7,96,192]{2,1,0:T(8,128)(2,1)} %param.12) | copy-start | bytes 774148
  43.1 2.6 copy-start.11
  43.1 3.0 copy-start.10
  43.1 3.3 copy-start.9
  43.5 3.3 copy-start.12
  43.5 3.3 copy-start.18
  43.5 3.3 copy-start.20
  43.5 3.3 copy-start.21
  159.2 4.6 copy-start
  161.0 5.4 %copy-start.2 = (f32[2,96,512]{1,2,0:T(8,128)}, f32[2,96,512]{1,2,0:T(8,128)S(1)}, u32[]{:S(2)}) copy-start(f32[2,96,512]{1,2,0:T(8,128)S(1)} %copy.143) | copy-start | bytes 1179652
  175.4 9.8 %copy-start.16 = (s32[12]{0:T(128)S(1)}, s32[12]{0:T(128)}, u32[]{:S(2)}) copy-start(s32[12]{0:T(128)} %reshape_squeeze.13) | copy-start | bytes 148
  178.3 16.3 %copy-start.1 = (f32[2,96,512]{1,2,0:T(8,128)S(1)}, f32[2,96,512]{1,2,0:T(8,128)}, u32[]{:S(2)}) copy-start(f32[2,96,512]{1,2,0:T(8,128)} %copy-done) | copy-start | bytes 1179652
  178.3 17.1 %copy-start.3 = (f32[2,96,512]{1,2,0:T(8,128)S(1)}, f32[2,96,512]{1,2,0:T(8,128)}, u32[]{:S(2)}) copy-start(f32[2,96,512]{1,2,0:T(8,128)} %copy-done.2) | copy-start | bytes 1179652
  178.3 18.0 %copy-start.4 = (f32[2,96,512]{1,2,0:T(8,128)S(1)}, f32[2,96,512]{1,2,0:T(8,128)}, u32[]{:S(2)}) copy-start(f32[2,96,512]{1,2,0:T(8,128)} %copy.145) | copy-start | bytes 1179652
  178.3 18.8 %copy-start.7 = (f32[2,96,512]{2,1,0:T(8,128)S(1)}, f32[2,96,512]{2,1,0:T(8,128)}, u32[]{:S(2)}) copy-start(f32[2,96,512]{2,1,0:T(8,128)} %convolution_bitcast_fusion.6) | copy-start | bytes 1179652
  185.2 17.5 %copy-start.17 = (pred[4,13]{1,0:T(4,128)(4,1)S(1)}, pred[4,13]{1,0:T(4,128)(4,1)}, u32[]{:S(2)}) copy-start(pred[4,13]{1,0:T(4,128)(4,1)} %iota_compare_fusion.2) | copy-start | bytes 160
  185.2 18.5 %copy-start.15 = (pred[4,13]{1,0:T(4,128)(4,1)S(1)}, pred[4,13]{1,0:T(4,128)(4,1)}, u32[]{:S(2)}) copy-start(pred[4,13]{1,0:T(4,128)(4,1)} %iota_compare_fusion.3) | copy-start | bytes 160
  188.3 14.4 %collective-permute-start.7 = (bf16[2,6144]{1,0:T(2,128)(2,1)}, bf16[2,6144]{1,0:T(2,128)(2,1)}, u32[]{:S(2)}, u32[]{:S(2)}) collective-permute-start(bf16[2,6144]{1,0:T(2,128)(2,1)} %get-tuple-element.20), channel_id=1, source_target_pairs={{0,1},{1,2},{2,3},{4,5},{5,6},{6,7},{8,9},{9,10},{10,11},{12,13},{... | collective-permute-start | bytes 73736 | tf_op jit(solution)/shard_map/ppermute | solution.py:18
  190.4 12.2 %collective-permute-start.6 = (bf16[2,6144]{1,0:T(2,128)(2,1)}, bf16[2,6144]{1,0:T(2,128)(2,1)}, u32[]{:S(2)}, u32[]{:S(2)}) collective-permute-start(bf16[2,6144]{1,0:T(2,128)(2,1)} %get-tuple-element.21), channel_id=1, source_target_pairs={{1,0},{2,1},{3,2},{5,4},{6,5},{7,6},{9,8},{10,9},{11,10},{13,12},{... | collective-permute-start | bytes 73736 | tf_op jit(solution)/shard_map/ppermute | solution.py:18
  194.6 2.8 copy-start.14
  194.6 4.1 copy-start.13
  195.4 15.5 %copy-start.5 = (f32[2,96,7,8,8]{1,4,3,2,0:T(8,128)S(1)}, f32[2,96,7,8,8]{1,4,3,2,0:T(8,128)}, u32[]{:S(2)}) copy-start(f32[2,96,7,8,8]{1,4,3,2,0:T(8,128)} %split.48) | copy-start | bytes 1032196
  197.0 13.9 %copy-start.6 = (f32[2,96,7,8,8]{1,4,3,2,0:T(8,128)S(1)}, f32[2,96,7,8,8]{1,4,3,2,0:T(8,128)}, u32[]{:S(2)}) copy-start(f32[2,96,7,8,8]{1,4,3,2,0:T(8,128)} %split.49) | copy-start | bytes 1032196
  197.3 6.4 %collective-permute-start.4 = (bf16[2,6144]{1,0:T(2,128)(2,1)S(1)}, bf16[2,6144]{1,0:T(2,128)(2,1)S(1)}, u32[]{:S(2)}, u32[]{:S(2)}) collective-permute-start(bf16[2,6144]{1,0:T(2,128)(2,1)S(1)} %copy-done.14), channel_id=1, source_target_pairs={{4,0},{8,4},{12,8},{16,12},{20,16},{24,20},{28,24},{32,28},{36,32}... | collective-permute-start | bytes 73736 | tf_op jit(solution)/shard_map/ppermute | solution.py:18
  198.7 5.1 %collective-permute-start.5 = (bf16[2,6144]{1,0:T(2,128)(2,1)S(1)}, bf16[2,6144]{1,0:T(2,128)(2,1)S(1)}, u32[]{:S(2)}, u32[]{:S(2)}) collective-permute-start(bf16[2,6144]{1,0:T(2,128)(2,1)S(1)} %copy-done.13), channel_id=1, source_target_pairs={{0,4},{4,8},{8,12},{12,16},{16,20},{20,24},{24,28},{28,32},{32,36}... | collective-permute-start | bytes 73736 | tf_op jit(solution)/shard_map/ppermute | solution.py:18
Sparse Core Ops, SparseCore 0:
  197.5 262.7 all-reduce.20
where the time goes:
time: 471 us; the launch traced here: 469 us
  waiting for transfers between devices  247 us (52%)
  blocking collectives  104 us (22%)
  local copies, waits for them, and re-layouts  45.1 us (10%)
  starting transfers between devices  26.8 us (6%)
  matrix products  19.5 us (4%)
  between operations  15.4 us (3%)
  other arithmetic  11.3 us (2%)
    psum x1, waiting for transfers between devices, local(): lax.psum((weight_terms, bias_terms), ('slab', 'cross'))  247 us
    psum x1, blocking collectives, local(): lax.psum((weight_terms, bias_terms), ('slab', 'cross'))  104 us
    ppermute x8, starting transfers between devices, shifted(): lax.ppermute(value, axis, [(source, source + steps) for source in range(i...  26.7 us
  transfers between devices with their start and end apart: 9, of which 1 were waited for; matrix products, arithmetic and copies ran while one was open for 5% of the time, Pallas kernels for 0%

commit v1 on v0

v1 whole, which is shorter than its diff:
```python
import math

import jax
import jax.numpy as jnp
from jax import lax
from jax.experimental import pallas as pl
from jax.experimental.pallas import tpu as pltpu
from jax.sharding import PartitionSpec as P

EDGE = 8
LAYER = EDGE * EDGE
TILE = 2 * LAYER
PACK = 16
f32 = jnp.float32
bf16 = jnp.bfloat16
VMEM = pl.BlockSpec(memory_space=pltpu.VMEM)
SMEM = pl.BlockSpec(memory_space=pltpu.SMEM)


def nn(a, b):
    return lax.dot_general(a, b, (((1,), (0,)), ((), ())), preferred_element_type=f32)


def nt(a, b):
    return lax.dot_general(a, b, (((1,), (1,)), ((), ())), preferred_element_type=f32)


def tn(a, b):
    return lax.dot_general(a, b, (((0,), (0,)), ((), ())), preferred_element_type=f32)


def layer_map(axis, voxels):
    row = lax.broadcasted_iota(jnp.int32, (TILE, voxels), 0)
    v = lax.broadcasted_iota(jnp.int32, (TILE, voxels), 1)
    x, y, z = v >> 6, (v >> 3) & 7, v & 7
    along, beside = (y, x * EDGE + z) if axis == 1 else (z, x * EDGE + y)
    low = (along == 0) & (row == beside)
    high = (along == EDGE - 1) & (row == beside + LAYER)
    return jnp.where(low | high, 1.0, 0.0).astype(bf16)


def low_half(rows):
    return lax.broadcasted_iota(jnp.int32, (rows, TILE), 1) < LAYER


def x_faces(brick):
    return jnp.where(low_half(brick.shape[0]), brick[:, :TILE], brick[:, -TILE:])


def doubled(tile):
    turned = pltpu.roll(tile, LAYER, 1)
    half = low_half(tile.shape[0])
    return jnp.where(half, tile, turned), jnp.where(half, turned, tile)


def send_kernel(features, slab_list, cross_list, *sends):
    number, channels, voxels = features.shape[2:]
    y_map = layer_map(1, voxels)
    half = low_half(channels)
    tables = ([], [])
    for b in range(number):
        brick = features[0, 0, b]
        tables[0].append(doubled(x_faces(brick.astype(f32))))
        tables[1].append(doubled(nt(brick, y_map)))
    for axis, listed in enumerate((slab_list, cross_list)):
        for row in range(2):
            side = 1 - row
            picked = []
            for k in range(2):
                entry = listed[0, 0, row, k]
                value = jnp.zeros((channels, TILE), f32)
                for b in range(number):
                    value = jnp.where(entry == 6 * b + 2 * axis + side, tables[axis][b][side], value)
                picked.append(value)
            sends[2 * axis + row][...] = jnp.where(half, picked[0], picked[1]).astype(bf16)


def main_kernel(features, upstream, weights, bias, count, links, slab_low, slab_high, cross_low, cross_high,
                back_slab_low, back_slab_high, back_cross_low, back_cross_high, terms, partial,
                fields, taps, table, grad, marks, table_grad):
    number, channels, voxels = features.shape[2:]
    out_channels = upstream.shape[3]
    depth = 7 * channels
    total = number * voxels
    own = 6 * number
    half = low_half(channels)
    lane = lax.broadcasted_iota(jnp.int32, (channels, total), 1)
    v = lane & (voxels - 1)
    coords = (v >> 6, (v >> 3) & 7, v & 7)
    strides = (LAYER, EDGE, 1)
    for axis in (1, 2):
        marks[TILE * (axis - 1):TILE * axis] = layer_map(axis, voxels)

    cubes = jnp.concatenate([features[0, 0, b] for b in range(number)], axis=1)
    cubes32 = cubes.astype(f32)
    for b in range(number):
        brick = features[0, 0, b]
        table[6 * b], table[6 * b + 1] = doubled(x_faces(brick.astype(f32)))
        sides = nt(brick, marks[...])
        table[6 * b + 2], table[6 * b + 3] = doubled(sides[:, :TILE])
        table[6 * b + 4], table[6 * b + 5] = doubled(sides[:, TILE:])
    for k, received in enumerate((slab_low, slab_high, cross_low, cross_high)):
        table[own + 2 * k], table[own + 2 * k + 1] = doubled(received[...].astype(f32))
    table[own + 8] = jnp.zeros((channels, TILE), f32)

    fields[:channels] = cubes
    for axis in range(3):
        expanded = []
        for b in range(number):
            tile = jnp.where(half, table[links[0, 0, b, 2 * axis]], table[links[0, 0, b, 2 * axis + 1]])
            if axis == 0:
                gap = jnp.zeros((channels, voxels - 2 * TILE), f32)
                expanded.append(jnp.concatenate([tile, gap, tile], axis=1))
            else:
                expanded.append(nn(tile.astype(bf16), marks[TILE * (axis - 1):TILE * axis]))
        outer = jnp.concatenate(expanded, axis=1)
        low = jnp.where(coords[axis] == 0, outer, pltpu.roll(cubes32, strides[axis], 1))
        high = jnp.where(coords[axis] == EDGE - 1, outer, pltpu.roll(cubes32, total - strides[axis], 1))
        fields[channels * (2 * axis + 1):channels * (2 * axis + 2)] = low.astype(bf16)
        fields[channels * (2 * axis + 2):channels * (2 * axis + 3)] = high.astype(bf16)
    fields[depth:] = jnp.ones((PACK, total), bf16)

    first = bias[...].astype(bf16)
    rest = bias[...] - first.astype(f32)
    second = rest.astype(bf16)
    third = (rest - second.astype(f32)).astype(bf16)
    row = lax.broadcasted_iota(jnp.int32, (PACK, out_channels), 0)
    extra = jnp.where(row == 0, first.astype(f32),
                      jnp.where(row == 1, second.astype(f32), jnp.where(row == 2, third.astype(f32), 0.0)))
    taps[:depth] = weights[...]
    taps[depth:] = extra.astype(bf16)

    pre = tn(taps[...], fields[...])
    grad[out_channels:] = jnp.zeros((grad.shape[0] - out_channels, total), bf16)
    for b in range(number):
        part = pre[:, voxels * b:voxels * (b + 1)]
        s = jax.nn.sigmoid(part)
        value = upstream[0, 0, b].astype(f32) * (s * (1.0 + part * (1.0 - s)))
        grad[:out_channels, voxels * b:voxels * (b + 1)] = jnp.where(b < count[0, 0], value, 0.0).astype(bf16)

    found = nt(fields[...], grad[...])
    middle = depth // 2
    terms[:depth] = found[:depth, :TILE].astype(bf16)
    terms[depth:depth + middle] = (found[:middle, TILE:] + pltpu.roll(found[middle:depth, TILE:], LAYER, 1)).astype(bf16)
    row = lax.broadcasted_iota(jnp.int32, (PACK, TILE), 0)
    terms[depth + middle:] = jnp.where(row == 0, found[depth:, :TILE],
                                       jnp.where(row == 1, found[depth:, TILE:], 0.0)).astype(bf16)

    table_grad[...] = jnp.zeros(table_grad.shape, f32)
    live = grad[:out_channels]
    summed = nn(weights[:channels], live)
    for axis in range(3):
        low = nn(weights[channels * (2 * axis + 1):channels * (2 * axis + 2)], live)
        high = nn(weights[channels * (2 * axis + 2):channels * (2 * axis + 3)], live)
        at = coords[axis]
        summed = summed + jnp.where(at < EDGE - 1, pltpu.roll(low, total - strides[axis], 1), 0.0)
        summed = summed + jnp.where(at > 0, pltpu.roll(high, strides[axis], 1), 0.0)
        edge = jnp.where(at == 0, low, high)
        for b in range(number):
            brick = edge[:, voxels * b:voxels * (b + 1)]
            if axis == 0:
                tile = x_faces(brick)
            else:
                tile = nt(brick.astype(bf16), marks[TILE * (axis - 1):TILE * axis])
            to_low, to_high = doubled(tile)
            table_grad[links[0, 0, b, 2 * axis]] = to_low
            table_grad[links[0, 0, b, 2 * axis + 1]] = to_high
    for k, back in enumerate((back_slab_low, back_slab_high, back_cross_low, back_cross_high)):
        back[...] = jnp.where(half, table_grad[own + 2 * k], table_grad[own + 2 * k + 1]).astype(bf16)
    for b in range(number):
        parts = summed[:, voxels * b:voxels * (b + 1)]
        for axis in range(3):
            tile = jnp.where(half, table_grad[6 * b + 2 * axis], table_grad[6 * b + 2 * axis + 1])
            parts = parts + spread(tile, axis, marks, voxels)
        partial[:, voxels * b:voxels * (b + 1)] = parts


def spread(tile, axis, marks, voxels):
    if axis > 0:
        return nn(tile.astype(bf16), marks[TILE * (axis - 1):TILE * axis])
    half = low_half(tile.shape[0])
    gap = jnp.zeros((tile.shape[0], voxels - 2 * TILE), f32)
    return jnp.concatenate([jnp.where(half, tile, 0.0), gap, jnp.where(half, 0.0, tile)], axis=1)


def sum_kernel(owners, partial, slab_list, cross_list, slab_first, slab_second, cross_first, cross_second,
               arrived, shared, result, marks):
    rows = arrived.shape[0]
    chunk = rows // owners
    step = max(chunk, PACK)
    value = jnp.sum(arrived[...].astype(f32).reshape(rows // step, step, TILE), axis=0)
    turn = chunk
    while turn < step:
        value = value + pltpu.roll(value, turn, 0)
        turn *= 2
    shared[...] = jnp.broadcast_to(value.astype(bf16)[None], (rows // step, step, TILE)).reshape(rows, TILE)

    number, channels, voxels = result.shape[2:]
    half = low_half(channels)
    marks[...] = layer_map(1, voxels)
    groups = ((slab_list, (slab_first, slab_second)), (cross_list, (cross_first, cross_second)))
    faces = [[doubled(back[...].astype(f32)) for back in backs] for _, backs in groups]
    for b in range(number):
        parts = partial[:, voxels * b:voxels * (b + 1)]
        for axis, (listed, _) in enumerate(groups):
            sides = []
            for side in range(2):
                value = jnp.zeros((channels, TILE), f32)
                for k in range(2):
                    entry = listed[0, 0, 1 - side, k]
                    value = value + jnp.where(entry == 6 * b + 2 * axis + side, faces[axis][1 - side][k], 0.0)
                sides.append(value)
            parts = parts + spread(jnp.where(half, sides[0], sides[1]), axis, marks, voxels)
        result[0, 0, b] = parts.astype(bf16)


def unpack_kernel(scale, gathered, kernel_grad, bias_grad):
    taps, channels, out_channels = kernel_grad.shape
    depth = taps * channels
    middle = depth // 2
    wide = gathered[...].astype(f32) * scale
    rest = wide[depth:depth + middle]
    second = jnp.concatenate([rest, pltpu.roll(rest, LAYER, 1)], axis=0)
    for tap in range(taps):
        rows = slice(channels * tap, channels * (tap + 1))
        kernel_grad[tap, :, :TILE] = wide[rows]
        kernel_grad[tap, :, TILE:] = second[rows, :out_channels - TILE]
    bias_grad[:, :TILE] = wide[depth + middle:depth + middle + 1]
    bias_grad[:, TILE:] = wide[depth + middle + 1:depth + middle + 2, :out_channels - TILE]


def shifted(value, axis, steps):
    count = lax.axis_size(axis)
    initial, last = (max(0, -steps), min(count, count - steps))
    return lax.ppermute(value, axis, [(source, source + steps) for source in range(initial, last)])


def shape(dims, dtype):
    return jax.ShapeDtypeStruct(dims, dtype)


def local(features, out_grad, weights, conv_bias, brick_count, neighbours, send_slab, send_cross):
    number, channels, voxels = features.shape[2:]
    out_channels = out_grad.shape[3]
    depth = 7 * channels
    total = number * voxels
    owners = lax.axis_size("slab") * lax.axis_size("cross")
    face_pair = shape((channels, TILE), bf16)
    limit = pltpu.CompilerParams(vmem_limit_bytes=48 * 2**20)

    sends = pl.pallas_call(
        send_kernel,
        out_shape=[face_pair] * 4,
        in_specs=[VMEM, SMEM, SMEM],
        out_specs=[VMEM] * 4,
        compiler_params=limit,
    )(features, send_slab, send_cross)
    slab_low = shifted(sends[0], "slab", 1)
    slab_high = shifted(sends[1], "slab", -1)
    cross_low = shifted(sends[2], "cross", 1)
    cross_high = shifted(sends[3], "cross", -1)

    packed = shape((depth * 3 // 2 + PACK, TILE), bf16)
    *backs, terms, partial = pl.pallas_call(
        main_kernel,
        out_shape=[face_pair] * 4 + [packed, shape((channels, total), f32)],
        in_specs=[VMEM] * 4 + [SMEM, SMEM] + [VMEM] * 4,
        out_specs=[VMEM] * 6,
        scratch_shapes=[
            pltpu.VMEM((depth + PACK, total), bf16),
            pltpu.VMEM((depth + PACK, out_channels), bf16),
            pltpu.VMEM((6 * number + 9, channels, TILE), f32),
            pltpu.VMEM((2 * TILE, total), bf16),
            pltpu.VMEM((2 * TILE, voxels), bf16),
            pltpu.VMEM((6 * number + 9, channels, TILE), f32),
        ],
        compiler_params=limit,
    )(features, out_grad, weights.reshape(depth, out_channels), conv_bias.reshape(1, out_channels), brick_count,
      neighbours, slab_low, slab_high, cross_low, cross_high)
    slab_first = shifted(backs[0], "slab", -1)
    slab_second = shifted(backs[1], "slab", 1)
    cross_first = shifted(backs[2], "cross", -1)
    cross_second = shifted(backs[3], "cross", 1)

    arrived = lax.all_to_all(terms, ("slab", "cross"), 0, 0, tiled=True)
    shared, grad_features = pl.pallas_call(
        lambda *refs: sum_kernel(owners, *refs),
        out_shape=[packed, shape(features.shape, bf16)],
        in_specs=[VMEM, SMEM, SMEM] + [VMEM] * 5,
        out_specs=[VMEM] * 2,
        scratch_shapes=[pltpu.VMEM((TILE, voxels), bf16)],
        compiler_params=limit,
    )(partial, send_slab, send_cross, slab_first, slab_second, cross_first, cross_second, arrived)
    gathered = lax.all_to_all(shared, ("slab", "cross"), 0, 0, tiled=True)
    scale = 1.0 / math.sqrt(owners * total)
    kernel_grad, bias_grad = pl.pallas_call(
        lambda *refs: unpack_kernel(scale, *refs),
        out_shape=[shape(weights.shape, f32), shape((1, out_channels), f32)],
        in_specs=[VMEM],
        out_specs=[VMEM] * 2,
        compiler_params=limit,
    )(gathered)
    return grad_features, kernel_grad, bias_grad.reshape(out_channels)


def solution(mesh):
    in_specs = (
        P("slab", "cross", None, None, None),
        P("slab", "cross", None, None, None),
        P(),
        P(),
        P("slab", "cross"),
        P("slab", "cross", None, None),
        P("slab", "cross", None, None),
        P("slab", "cross", None, None),
    )
    out_specs = (P("slab", "cross", None, None, None), P(), P())
    return jax.shard_map(local, mesh=mesh, in_specs=in_specs, out_specs=out_specs, check_vma=False)
```

time: 471 us -> 103 us (0.22)
  waiting for transfers between devices: 247 us -> 4.21 us
  blocking collectives: 104 us -> 35.1 us
  local copies, waits for them, and re-layouts: 45.1 us -> 5.62 us
  starting transfers between devices: 26.8 us -> 49.4 us
  matrix products: 19.5 us -> 0 us
  between operations: 15.4 us -> 1.46 us
  other arithmetic: 11.3 us -> 0 us
  Pallas kernels: 0 us -> 7.03 us
    psum x1 -> x0, waiting for transfers between devices: 247 us -> none  [local(): lax.psum((weight_terms, bias_terms), ('slab', 'cross'))]
    psum x1 -> x0, blocking collectives: 104 us -> none  [local(): lax.psum((weight_terms, bias_terms), ('slab', 'cross'))]
    all_to_all x0 -> x1, blocking collectives: none -> 35.1 us  [local(): gathered = lax.all_to_all(shared, ('slab', 'cross'), 0, 0, tiled=True)]
    all_to_all x0 -> x1, starting transfers between devices: none -> 22.8 us  [local(): arrived = lax.all_to_all(terms, ('slab', 'cross'), 0, 0, tiled=True)]
    dot_general x24 -> x0, matrix products: 19.5 us -> none  [the longest x7 6.25 us: local(): jnp.einsum('biv,bov->io', fields[tap_index], grad_pre, preferred_element_...]
    reshape x3 -> x0, local copies, waits for them, and re-layouts: 8.39 us -> none  [the longest x1 6.93 us: local(): grad_beside.reshape(local_rows, row_width)]
    pallas_call x0 -> x4, Pallas kernels: none -> 7.03 us  [the longest x1 3.53 us: local(): pl.pallas_call(main_kernel, out_shape=[face_pair] * 4 + [packed, shape((c...]
    transpose x7 -> x0, local copies, waits for them, and re-layouts: 6.14 us -> none  [local(): jnp.einsum('io,bov->biv', weights[tap_index], grad_pre, preferred_element...]
  transfers between devices with their start and end apart: 9 -> 9, of which waited for: 1 -> 3; matrix products, arithmetic and copies ran while one was open for 5% -> 0% of each run, Pallas kernels for 0% -> 0%
where the time goes in v1:
time: 103 us
  starting transfers between devices  49.4 us (48%)
  blocking collectives  35.1 us (34%)
  Pallas kernels  7.03 us (7%)
  local copies, waits for them, and re-layouts  5.62 us (5%)
  waiting for transfers between devices  4.21 us (4%)
  between operations  1.46 us (1%)
    all_to_all x1, blocking collectives, local(): gathered = lax.all_to_all(shared, ('slab', 'cross'), 0, 0, tiled=True)  35.1 us
    ppermute x8, starting transfers between devices, shifted(): lax.ppermute(value, axis, [(source, source + steps) for source in range(i...  26.6 us
    all_to_all x1, starting transfers between devices, local(): arrived = lax.all_to_all(terms, ('slab', 'cross'), 0, 0, tiled=True)  22.8 us
    unnamed x18, local copies, waits for them, and re-layouts  5.62 us
    pallas_call x1, Pallas kernels, local(): pl.pallas_call(main_kernel, out_shape=[face_pair] * 4 + [packed, shape((c...  3.53 us
    ppermute x8, waiting for transfers between devices, shifted(): lax.ppermute(value, axis, [(source, source + steps) for source in range(i...  2.2 us
  transfers between devices with their start and end apart: 9, of which 3 were waited for; matrix products, arithmetic and copies ran while one was open for 0% of the time, Pallas kernels for 0%

profile of v1, /device:TPU:1, one launch (start us, length us, event | category | flops | bytes accessed | tf_op | source)
XLA Modules:
  0.0 102.8 jit_solution(18233258943199913544)
XLA Ops:
  0.6 0.0 copy-start
  0.6 0.9 copy-done
  1.6 0.0 copy-start.3
  1.6 0.7 copy-done.3
  2.2 0.0 copy-start.5
  2.2 0.7 copy-done.5
  2.9 0.9 shard_map.103
  3.9 3.9 %collective-permute-start = (bf16[96,128]{1,0:T(8,128)(2,1)S(1)}, bf16[96,128]{1,0:T(8,128)(2,1)S(1)}, u32[]{:S(2)}, u32[]{:S(2)}) collective-permute-start(bf16[96,128]{1,0:T(8,128)(2,1)S(1)} %get-tuple-element.17), channel_id=1, source_target_pairs={{0,4},{4,8},{8,12},{12,16},{16,20},{20,24},{24,28},{28,32},{32,36}... | collective-permute-start | bytes 73736 | tf_op jit(solution)/shard_map/ppermute | solution.py:235
  7.8 1.3 %collective-permute-start.1 = (bf16[96,128]{1,0:T(8,128)(2,1)S(1)}, bf16[96,128]{1,0:T(8,128)(2,1)S(1)}, u32[]{:S(2)}, u32[]{:S(2)}) collective-permute-start(bf16[96,128]{1,0:T(8,128)(2,1)S(1)} %get-tuple-element.18), channel_id=1, source_target_pairs={{4,0},{8,4},{12,8},{16,12},{20,16},{24,20},{28,24},{32,28},{36,32}... | collective-permute-start | bytes 73736 | tf_op jit(solution)/shard_map/ppermute | solution.py:235
  9.1 4.0 %collective-permute-start.2 = (bf16[96,128]{1,0:T(8,128)(2,1)S(1)}, bf16[96,128]{1,0:T(8,128)(2,1)S(1)}, u32[]{:S(2)}, u32[]{:S(2)}) collective-permute-start(bf16[96,128]{1,0:T(8,128)(2,1)S(1)} %get-tuple-element.19), channel_id=1, source_target_pairs={{0,1},{1,2},{2,3},{4,5},{5,6},{6,7},{8,9},{9,10},{10,11},{12,13},{... | collective-permute-start | bytes 73736 | tf_op jit(solution)/shard_map/ppermute | solution.py:235
  13.2 3.4 %collective-permute-start.3 = (bf16[96,128]{1,0:T(8,128)(2,1)S(1)}, bf16[96,128]{1,0:T(8,128)(2,1)S(1)}, u32[]{:S(2)}, u32[]{:S(2)}) collective-permute-start(bf16[96,128]{1,0:T(8,128)(2,1)S(1)} %get-tuple-element.20), channel_id=1, source_target_pairs={{1,0},{2,1},{3,2},{5,4},{6,5},{7,6},{9,8},{10,9},{11,10},{13,12},{... | collective-permute-start | bytes 73736 | tf_op jit(solution)/shard_map/ppermute | solution.py:235
  16.6 0.0 copy-start.8
  17.2 0.0 collective-permute-done.slab_low
  17.2 0.0 collective-permute-done.1.slab_high
  17.2 0.0 collective-permute-done.2.cross_low
  17.3 1.1 %collective-permute-done.3.cross_high = bf16[96,128]{1,0:T(8,128)(2,1)S(1)} collective-permute-done((bf16[96,128]{1,0:T(8,128)(2,1)S(1)}, bf16[96,128]{1,0:T(8,128)(2,1)S(1)}, u32[]{:S(2)}, u32[]{:S(2)}) %collective-permute-start.3) | collective-permute-done | bytes 24608 | tf_op jit(solution)/shard_map/ppermute | solution.py:235
  18.3 0.0 copy-start.7
  18.3 0.0 copy-done.8
  18.3 0.7 copy-done.7
  19.0 0.0 copy-start.1
  19.0 1.0 copy-done.1
  20.0 0.0 copy-start.2
  20.0 1.0 copy-done.2
  21.0 3.5 %shard_map.104 = (bf16[96,128]{1,0:T(8,128)(2,1)S(1)}, bf16[96,128]{1,0:T(8,128)(2,1)S(1)}, bf16[96,128]{1,0:T(8,128)(2,1)S(1)}, bf16[96,128]{1,0:T(8,128)(2,1)S...) custom-call(bf16[1,1,2,96,512]{4,3,2,1,0:T(8,128)(2,1)S(1)} %copy-done, ...), custom_call_target="tpu_custom_call" | custom-call | tf_op jit(solution)/shard_map/pallas_call | solution.py:264
  24.5 0.0 copy-start.6
  24.5 22.8 %all-to-all-start = ((bf16[512,2,128]{2,1,0:T(2,128)(2,1)}), bf16[512,2,128]{2,1,0:T(2,128)(2,1)S(1)}, u32[]{:S(2)}, u32[]{:S(2)}) async-start(bf16[512,2,128]{2,1,0:T(2,128)(2,1)} %bitcast.2), calls=%async_computation | async-start | bytes 524288 | tf_op jit(solution)/shard_map/all_to_all | solution.py:285
  47.3 1.3 %collective-permute-start.4 = (bf16[96,128]{1,0:T(8,128)(2,1)S(1)}, bf16[96,128]{1,0:T(8,128)(2,1)S(1)}, u32[]{:S(2)}, u32[]{:S(2)}) collective-permute-start(bf16[96,128]{1,0:T(8,128)(2,1)S(1)} %get-tuple-element.22), channel_id=1, source_target_pairs={{4,0},{8,4},{12,8},{16,12},{20,16},{24,20},{28,24},{32,28},{36,32}... | collective-permute-start | bytes 73736 | tf_op jit(solution)/shard_map/ppermute | solution.py:235
  48.6 4.0 %collective-permute-start.5 = (bf16[96,128]{1,0:T(8,128)(2,1)S(1)}, bf16[96,128]{1,0:T(8,128)(2,1)S(1)}, u32[]{:S(2)}, u32[]{:S(2)}) collective-permute-start(bf16[96,128]{1,0:T(8,128)(2,1)S(1)} %get-tuple-element.23), channel_id=1, source_target_pairs={{0,4},{4,8},{8,12},{12,16},{16,20},{20,24},{24,28},{28,32},{32,36}... | collective-permute-start | bytes 73736 | tf_op jit(solution)/shard_map/ppermute | solution.py:235
  52.6 6.8 %collective-permute-start.6 = (bf16[96,128]{1,0:T(8,128)(2,1)S(1)}, bf16[96,128]{1,0:T(8,128)(2,1)S(1)}, u32[]{:S(2)}, u32[]{:S(2)}) collective-permute-start(bf16[96,128]{1,0:T(8,128)(2,1)S(1)} %get-tuple-element.24), channel_id=1, source_target_pairs={{1,0},{2,1},{3,2},{5,4},{6,5},{7,6},{9,8},{10,9},{11,10},{13,12},{... | collective-permute-start | bytes 73736 | tf_op jit(solution)/shard_map/ppermute | solution.py:235
  59.4 1.9 %collective-permute-start.7 = (bf16[96,128]{1,0:T(8,128)(2,1)S(1)}, bf16[96,128]{1,0:T(8,128)(2,1)S(1)}, u32[]{:S(2)}, u32[]{:S(2)}) collective-permute-start(bf16[96,128]{1,0:T(8,128)(2,1)S(1)} %get-tuple-element.25), channel_id=1, source_target_pairs={{0,1},{1,2},{2,3},{4,5},{5,6},{6,7},{8,9},{9,10},{10,11},{12,13},{... | collective-permute-start | bytes 73736 | tf_op jit(solution)/shard_map/ppermute | solution.py:235
  61.3 0.0 collective-permute-done.4.refs_3_
  61.3 0.0 collective-permute-done.5.refs_4_
  61.3 0.0 collective-permute-done.6.refs_5_
  61.3 1.1 %collective-permute-done.7.refs_6_ = bf16[96,128]{1,0:T(8,128)(2,1)S(1)} collective-permute-done((bf16[96,128]{1,0:T(8,128)(2,1)S(1)}, bf16[96,128]{1,0:T(8,128)(2,1)S(1)}, u32[]{:S(2)}, u32[]{:S(2)}) %collective-permute-start.7) | collective-permute-done | bytes 24608 | tf_op jit(solution)/shard_map/ppermute | solution.py:235
  62.5 2.0 %all-to-all-done = bf16[512,2,128]{2,1,0:T(2,128)(2,1)S(1)} async-done(((bf16[512,2,128]{2,1,0:T(2,128)(2,1)}), bf16[512,2,128]{2,1,0:T(2,128)(2,1)S(1)}, u32[]{:S(2)}, u32[]{:S(2)}) %all-to-all-start) | async-done | bytes 262176 | tf_op jit(solution)/shard_map/all_to_all | solution.py:285
  64.5 0.0 copy-start.4
  64.5 0.0 copy-done.6
  64.5 0.7 copy-done.4
  65.2 1.6 %shard_map.105 = (bf16[1024,128]{1,0:T(8,128)(2,1)S(1)}, bf16[1,1,2,96,512]{4,3,2,1,0:T(8,128)(2,1)}) custom-call(f32[96,1024]{1,0:T(8,128)S(1)} %get-tuple-element.21.refs_0_, s32[1,1,2,2]{3,2,1,0:T(2,128)S(1)} %copy-done.4, s32[1,1,2,2]{3,2,1,0:T(2,128)S(1)} %copy-done.6, bf16[96,128]{1,0:T(8,128)(2,1)S(1)} %collective-permute-done.4.refs_3_, ...), custom_call_target="tpu_custom_call" | custom-call | tf_op jit(solution)/shard_map/pallas_call | solution.py:286
  66.8 35.1 %all_to_all.22 = bf16[512,2,128]{2,1,0:T(2,128)(2,1)S(1)} all-to-all(bf16[512,2,128]{2,1,0:T(2,128)(2,1)S(1)} %bitcast.10), channel_id=1, replica_groups=mesh['slab'=128,'cross'=4] {'slab','cross'}, dimensions={0} | all-to-all | bytes 524288 | tf_op jit(solution)/shard_map/all_to_all | solution.py:294
  101.8 1.0 shard_map.106
Async XLA Ops:
  0.6 0.9 copy-start
  1.6 0.7 copy-start.3
  2.2 0.7 copy-start.5
  3.9 13.4 %collective-permute-start = (bf16[96,128]{1,0:T(8,128)(2,1)S(1)}, bf16[96,128]{1,0:T(8,128)(2,1)S(1)}, u32[]{:S(2)}, u32[]{:S(2)}) collective-permute-start(bf16[96,128]{1,0:T(8,128)(2,1)S(1)} %get-tuple-element.17), channel_id=1, source_target_pairs={{0,4},{4,8},{8,12},{12,16},{16,20},{20,24},{24,28},{28,32},{32,36}... | collective-permute-start | bytes 73736 | tf_op jit(solution)/shard_map/ppermute | solution.py:235
  7.8 9.4 %collective-permute-start.1 = (bf16[96,128]{1,0:T(8,128)(2,1)S(1)}, bf16[96,128]{1,0:T(8,128)(2,1)S(1)}, u32[]{:S(2)}, u32[]{:S(2)}) collective-permute-start(bf16[96,128]{1,0:T(8,128)(2,1)S(1)} %get-tuple-element.18), channel_id=1, source_target_pairs={{4,0},{8,4},{12,8},{16,12},{20,16},{24,20},{28,24},{32,28},{36,32}... | collective-permute-start | bytes 73736 | tf_op jit(solution)/shard_map/ppermute | solution.py:235
  9.1 8.1 %collective-permute-start.2 = (bf16[96,128]{1,0:T(8,128)(2,1)S(1)}, bf16[96,128]{1,0:T(8,128)(2,1)S(1)}, u32[]{:S(2)}, u32[]{:S(2)}) collective-permute-start(bf16[96,128]{1,0:T(8,128)(2,1)S(1)} %get-tuple-element.19), channel_id=1, source_target_pairs={{0,1},{1,2},{2,3},{4,5},{5,6},{6,7},{8,9},{9,10},{10,11},{12,13},{... | collective-permute-start | bytes 73736 | tf_op jit(solution)/shard_map/ppermute | solution.py:235
  13.2 5.1 %collective-permute-start.3 = (bf16[96,128]{1,0:T(8,128)(2,1)S(1)}, bf16[96,128]{1,0:T(8,128)(2,1)S(1)}, u32[]{:S(2)}, u32[]{:S(2)}) collective-permute-start(bf16[96,128]{1,0:T(8,128)(2,1)S(1)} %get-tuple-element.20), channel_id=1, source_target_pairs={{1,0},{2,1},{3,2},{5,4},{6,5},{7,6},{9,8},{10,9},{11,10},{13,12},{... | collective-permute-start | bytes 73736 | tf_op jit(solution)/shard_map/ppermute | solution.py:235
  16.6 1.8 %copy-start.8 = (s32[1,1,2,6]{3,2,1,0:T(2,128)S(1)}, s32[1,1,2,6]{3,2,1,0:T(2,128)}, u32[]{:S(2)}) copy-start(s32[1,1,2,6]{3,2,1,0:T(2,128)} %links.1) | copy-start | bytes 148
  18.3 0.7 copy-start.7
  19.0 1.0 copy-start.1
  20.0 1.0 copy-start.2
  24.5 40.0 %copy-start.6 = (s32[1,1,2,2]{3,2,1,0:T(2,128)S(1)}, s32[1,1,2,2]{3,2,1,0:T(2,128)}, u32[]{:S(2)}) copy-start(s32[1,1,2,2]{3,2,1,0:T(2,128)} %refs_2_.1) | copy-start | bytes 52
  24.5 40.0 %all-to-all-start = ((bf16[512,2,128]{2,1,0:T(2,128)(2,1)}), bf16[512,2,128]{2,1,0:T(2,128)(2,1)S(1)}, u32[]{:S(2)}, u32[]{:S(2)}) async-start(bf16[512,2,128]{2,1,0:T(2,128)(2,1)} %bitcast.2), calls=%async_computation | async-start | bytes 524288 | tf_op jit(solution)/shard_map/all_to_all | solution.py:285
  47.3 14.0 %collective-permute-start.4 = (bf16[96,128]{1,0:T(8,128)(2,1)S(1)}, bf16[96,128]{1,0:T(8,128)(2,1)S(1)}, u32[]{:S(2)}, u32[]{:S(2)}) collective-permute-start(bf16[96,128]{1,0:T(8,128)(2,1)S(1)} %get-tuple-element.22), channel_id=1, source_target_pairs={{4,0},{8,4},{12,8},{16,12},{20,16},{24,20},{28,24},{32,28},{36,32}... | collective-permute-start | bytes 73736 | tf_op jit(solution)/shard_map/ppermute | solution.py:235
  48.6 12.7 %collective-permute-start.5 = (bf16[96,128]{1,0:T(8,128)(2,1)S(1)}, bf16[96,128]{1,0:T(8,128)(2,1)S(1)}, u32[]{:S(2)}, u32[]{:S(2)}) collective-permute-start(bf16[96,128]{1,0:T(8,128)(2,1)S(1)} %get-tuple-element.23), channel_id=1, source_target_pairs={{0,4},{4,8},{8,12},{12,16},{16,20},{20,24},{24,28},{28,32},{32,36}... | collective-permute-start | bytes 73736 | tf_op jit(solution)/shard_map/ppermute | solution.py:235
  52.6 8.7 %collective-permute-start.6 = (bf16[96,128]{1,0:T(8,128)(2,1)S(1)}, bf16[96,128]{1,0:T(8,128)(2,1)S(1)}, u32[]{:S(2)}, u32[]{:S(2)}) collective-permute-start(bf16[96,128]{1,0:T(8,128)(2,1)S(1)} %get-tuple-element.24), channel_id=1, source_target_pairs={{1,0},{2,1},{3,2},{5,4},{6,5},{7,6},{9,8},{10,9},{11,10},{13,12},{... | collective-permute-start | bytes 73736 | tf_op jit(solution)/shard_map/ppermute | solution.py:235
  59.4 3.1 %collective-permute-start.7 = (bf16[96,128]{1,0:T(8,128)(2,1)S(1)}, bf16[96,128]{1,0:T(8,128)(2,1)S(1)}, u32[]{:S(2)}, u32[]{:S(2)}) collective-permute-start(bf16[96,128]{1,0:T(8,128)(2,1)S(1)} %get-tuple-element.25), channel_id=1, source_target_pairs={{0,1},{1,2},{2,3},{4,5},{5,6},{6,7},{8,9},{9,10},{10,11},{12,13},{... | collective-permute-start | bytes 73736 | tf_op jit(solution)/shard_map/ppermute | solution.py:235
  64.5 0.7 copy-start.4

commit v2 on v1

--- a/solution.py
+++ b/solution.py
@@ -11,10 +11,14 @@
 LAYER = EDGE * EDGE
 TILE = 2 * LAYER
 PACK = 16
+FIRST = 60 * 2**20
+MIDDLE = 56_000_000
+NEAR = (0, 1, 2, 3, 6)
 f32 = jnp.float32
 bf16 = jnp.bfloat16
 VMEM = pl.BlockSpec(memory_space=pltpu.VMEM)
 SMEM = pl.BlockSpec(memory_space=pltpu.SMEM)
+HBM = pl.BlockSpec(memory_space=pltpu.HBM)
 
 
 def nn(a, b):
@@ -53,15 +57,43 @@
     return jnp.where(half, tile, turned), jnp.where(half, turned, tile)
 
 
-def send_kernel(features, slab_list, cross_list, *sends):
+def fetch(sources, targets, arrivals):
+    copies = [pltpu.make_async_copy(a, b, arrivals.at[k]) for k, (a, b) in enumerate(zip(sources, targets))]
+    for copy in copies:
+        copy.start()
+    return copies
+
+
+def choose(axis, even, odd):
+    return jnp.where((lax.axis_index(axis) & 1) == 0, even, odd)
+
+
+def to_peers(refs, up, down, cross_up, cross_down):
+    for ref, tile in zip(refs, (choose("slab", down, up), choose("slab", up, down),
+                                choose("cross", cross_down, cross_up), choose("cross", cross_up, cross_down))):
+        ref[...] = tile.astype(bf16)
+
+
+def from_peers(refs):
+    far, near, cross_far, cross_near = [ref[...].astype(f32) for ref in refs]
+    return (choose("slab", far, near), choose("slab", near, far),
+            choose("cross", cross_far, cross_near), choose("cross", cross_near, cross_far))
+
+
+def send_kernel(features_in, slab_in, cross_in, *refs):
+    faces, (features, slab_list, cross_list, arrivals) = refs[:4], refs[4:]
+    copies = fetch((features_in, slab_in, cross_in), (features, slab_list, cross_list), arrivals)
     number, channels, voxels = features.shape[2:]
     y_map = layer_map(1, voxels)
+    for copy in copies:
+        copy.wait()
     half = low_half(channels)
     tables = ([], [])
     for b in range(number):
         brick = features[0, 0, b]
         tables[0].append(doubled(x_faces(brick.astype(f32))))
         tables[1].append(doubled(nt(brick, y_map)))
+    sends = []
     for axis, listed in enumerate((slab_list, cross_list)):
         for row in range(2):
             side = 1 - row
@@ -72,12 +104,16 @@
                 for b in range(number):
                     value = jnp.where(entry == 6 * b + 2 * axis + side, tables[axis][b][side], value)
                 picked.append(value)
-            sends[2 * axis + row][...] = jnp.where(half, picked[0], picked[1]).astype(bf16)
-
-
-def main_kernel(features, upstream, weights, bias, count, links, slab_low, slab_high, cross_low, cross_high,
-                back_slab_low, back_slab_high, back_cross_low, back_cross_high, terms, partial,
-                fields, taps, table, grad, marks, table_grad):
+            sends.append(jnp.where(half, picked[0], picked[1]))
+    to_peers(faces, *sends)
+
+
+def main_kernel(features_in, weights_in, upstream_in, bias_in, count_in, links_in, *refs):
+    received, sent, (terms, partial), refs = refs[:4], refs[4:8], refs[8:10], refs[10:]
+    features, weights, upstream, bias, count, links, fields, grad, taps, table, marks, table_grad, arrivals = refs
+    copies = fetch(
+        (features_in, links_in, weights_in, bias_in, count_in, upstream_in),
+        (features, links, weights, bias, count, upstream), arrivals)
     number, channels, voxels = features.shape[2:]
     out_channels = upstream.shape[3]
     depth = 7 * channels
@@ -90,6 +126,7 @@
     strides = (LAYER, EDGE, 1)
     for axis in (1, 2):
         marks[TILE * (axis - 1):TILE * axis] = layer_map(axis, voxels)
+    copies[0].wait()
 
     cubes = jnp.concatenate([features[0, 0, b] for b in range(number)], axis=1)
     cubes32 = cubes.astype(f32)
@@ -99,8 +136,9 @@
         sides = nt(brick, marks[...])
         table[6 * b + 2], table[6 * b + 3] = doubled(sides[:, :TILE])
         table[6 * b + 4], table[6 * b + 5] = doubled(sides[:, TILE:])
-    for k, received in enumerate((slab_low, slab_high, cross_low, cross_high)):
-        table[own + 2 * k], table[own + 2 * k + 1] = doubled(received[...].astype(f32))
+    for k, tile in enumerate(from_peers(received)):
+        table[own + 2 * k], table[own + 2 * k + 1] = doubled(tile)
+    copies[1].wait()
     table[own + 8] = jnp.zeros((channels, TILE), f32)
 
     fields[:channels] = cubes
@@ -120,6 +158,8 @@
         fields[channels * (2 * axis + 2):channels * (2 * axis + 3)] = high.astype(bf16)
     fields[depth:] = jnp.ones((PACK, total), bf16)
 
+    copies[2].wait()
+    copies[3].wait()
     first = bias[...].astype(bf16)
     rest = bias[...] - first.astype(f32)
     second = rest.astype(bf16)
@@ -131,6 +171,8 @@
     taps[depth:] = extra.astype(bf16)
 
     pre = tn(taps[...], fields[...])
+    copies[4].wait()
+    copies[5].wait()
     grad[out_channels:] = jnp.zeros((grad.shape[0] - out_channels, total), bf16)
     for b in range(number):
         part = pre[:, voxels * b:voxels * (b + 1)]
@@ -165,8 +207,9 @@
             to_low, to_high = doubled(tile)
             table_grad[links[0, 0, b, 2 * axis]] = to_low
             table_grad[links[0, 0, b, 2 * axis + 1]] = to_high
-    for k, back in enumerate((back_slab_low, back_slab_high, back_cross_low, back_cross_high)):
-        back[...] = jnp.where(half, table_grad[own + 2 * k], table_grad[own + 2 * k + 1]).astype(bf16)
+    low, high, cross_low, cross_high = [
+        jnp.where(half, table_grad[own + 2 * k], table_grad[own + 2 * k + 1]) for k in range(4)]
+    to_peers(sent, high, low, cross_high, cross_low)
     for b in range(number):
         parts = summed[:, voxels * b:voxels * (b + 1)]
         for axis in range(3):
@@ -183,23 +226,23 @@
     return jnp.concatenate([jnp.where(half, tile, 0.0), gap, jnp.where(half, 0.0, tile)], axis=1)
 
 
-def sum_kernel(owners, partial, slab_list, cross_list, slab_first, slab_second, cross_first, cross_second,
-               arrived, shared, result, marks):
-    rows = arrived.shape[0]
-    chunk = rows // owners
-    step = max(chunk, PACK)
-    value = jnp.sum(arrived[...].astype(f32).reshape(rows // step, step, TILE), axis=0)
-    turn = chunk
-    while turn < step:
-        value = value + pltpu.roll(value, turn, 0)
-        turn *= 2
-    shared[...] = jnp.broadcast_to(value.astype(bf16)[None], (rows // step, step, TILE)).reshape(rows, TILE)
-
+def sum_chunks(arrived, shared, parts):
+    rows = shared.shape[0] // parts
+    value = jnp.sum(arrived[...].astype(f32).reshape(arrived.shape[0] // rows, rows, TILE), axis=0).astype(bf16)
+    shared[...] = jnp.broadcast_to(value[None], (parts, rows, TILE)).reshape(shared.shape)
+
+
+def finish_kernel(parts, partial, slab_in, cross_in, slab_far, slab_near, cross_far, cross_near, arrived, shared, result, marks, slab_list, cross_list, arrivals):
+    copies = fetch((slab_in, cross_in), (slab_list, cross_list), arrivals)
+    sum_chunks(arrived, shared, parts)
     number, channels, voxels = result.shape[2:]
     half = low_half(channels)
     marks[...] = layer_map(1, voxels)
-    groups = ((slab_list, (slab_first, slab_second)), (cross_list, (cross_first, cross_second)))
-    faces = [[doubled(back[...].astype(f32)) for back in backs] for _, backs in groups]
+    for copy in copies:
+        copy.wait()
+    second, first, cross_second, cross_first = from_peers((slab_far, slab_near, cross_far, cross_near))
+    groups = ((slab_list, (first, second)), (cross_list, (cross_first, cross_second)))
+    faces = [[doubled(back) for back in backs] for _, backs in groups]
     for b in range(number):
         parts = partial[:, voxels * b:voxels * (b + 1)]
         for axis, (listed, _) in enumerate(groups):
@@ -229,10 +272,25 @@
     bias_grad[:, TILE:] = wide[depth + middle + 1:depth + middle + 2, :out_channels - TILE]
 
 
-def shifted(value, axis, steps):
-    count = lax.axis_size(axis)
-    initial, last = (max(0, -steps), min(count, count - steps))
-    return lax.ppermute(value, axis, [(source, source + steps) for source in range(initial, last)])
+def groups_of(bits, count):
+    mask = sum(1 << bit for bit in bits)
+    found = {}
+    for device in range(count):
+        found.setdefault(device & ~mask, []).append(device)
+    return list(found.values())
+
+
+def swap(slab_far, slab_near, cross_far, cross_near):
+    def pairs(value, axis, first):
+        lows = range(first, lax.axis_size(axis) - 1, 2)
+        return lax.ppermute(value, axis, [pair for low in lows for pair in ((low, low + 1), (low + 1, low))])
+
+    return (pairs(slab_far, "slab", 1), pairs(slab_near, "slab", 0),
+            pairs(cross_far, "cross", 1), pairs(cross_near, "cross", 0))
+
+
+def exchange(value, bits, count):
+    return lax.all_to_all(value, ("slab", "cross"), 0, 0, axis_index_groups=groups_of(bits, count), tiled=True)
 
 
 def shape(dims, dtype):
@@ -246,59 +304,79 @@
     total = number * voxels
     owners = lax.axis_size("slab") * lax.axis_size("cross")
     face_pair = shape((channels, TILE), bf16)
-    limit = pltpu.CompilerParams(vmem_limit_bytes=48 * 2**20)
+    limit = pltpu.CompilerParams(vmem_limit_bytes=FIRST)
+    middle = pltpu.CompilerParams(vmem_limit_bytes=MIDDLE)
+    small = pltpu.CompilerParams(vmem_limit_bytes=16 * 2**20)
 
     sends = pl.pallas_call(
         send_kernel,
         out_shape=[face_pair] * 4,
-        in_specs=[VMEM, SMEM, SMEM],
+        in_specs=[HBM] * 3,
         out_specs=[VMEM] * 4,
+        scratch_shapes=[
+            pltpu.VMEM(features.shape, bf16),
+            pltpu.SMEM(send_slab.shape, jnp.int32),
+            pltpu.SMEM(send_cross.shape, jnp.int32),
+            pltpu.SemaphoreType.DMA((3,)),
+        ],
         compiler_params=limit,
     )(features, send_slab, send_cross)
-    slab_low = shifted(sends[0], "slab", 1)
-    slab_high = shifted(sends[1], "slab", -1)
-    cross_low = shifted(sends[2], "cross", 1)
-    cross_high = shifted(sends[3], "cross", -1)
-
     packed = shape((depth * 3 // 2 + PACK, TILE), bf16)
     *backs, terms, partial = pl.pallas_call(
         main_kernel,
         out_shape=[face_pair] * 4 + [packed, shape((channels, total), f32)],
-        in_specs=[VMEM] * 4 + [SMEM, SMEM] + [VMEM] * 4,
+        in_specs=[HBM] * 6 + [VMEM] * 4,
         out_specs=[VMEM] * 6,
         scratch_shapes=[
+            pltpu.VMEM(features.shape, bf16),
+            pltpu.VMEM((depth, out_channels), bf16),
+            pltpu.VMEM(out_grad.shape, bf16),
+            pltpu.VMEM((1, out_channels), f32),
+            pltpu.SMEM(brick_count.shape, jnp.int32),
+            pltpu.SMEM(neighbours.shape, jnp.int32),
             pltpu.VMEM((depth + PACK, total), bf16),
+            pltpu.VMEM((2 * TILE, total), bf16),
             pltpu.VMEM((depth + PACK, out_channels), bf16),
             pltpu.VMEM((6 * number + 9, channels, TILE), f32),
-            pltpu.VMEM((2 * TILE, total), bf16),
             pltpu.VMEM((2 * TILE, voxels), bf16),
             pltpu.VMEM((6 * number + 9, channels, TILE), f32),
+            pltpu.SemaphoreType.DMA((6,)),
         ],
-        compiler_params=limit,
-    )(features, out_grad, weights.reshape(depth, out_channels), conv_bias.reshape(1, out_channels), brick_count,
-      neighbours, slab_low, slab_high, cross_low, cross_high)
-    slab_first = shifted(backs[0], "slab", -1)
-    slab_second = shifted(backs[1], "slab", 1)
-    cross_first = shifted(backs[2], "cross", -1)
-    cross_second = shifted(backs[3], "cross", 1)
-
-    arrived = lax.all_to_all(terms, ("slab", "cross"), 0, 0, tiled=True)
+        compiler_params=middle,
+    )(features, weights.reshape(depth, out_channels), out_grad, conv_bias.reshape(1, out_channels), brick_count,
+      neighbours, *swap(*sends))
+    returned = swap(*backs)
+
+    near = NEAR if owners == 512 else tuple(range(owners.bit_length() // 2))
+    far = tuple(bit for bit in range(owners.bit_length() - 1) if bit not in near)
+    arrived = exchange(terms, near, owners)
+    shared = pl.pallas_call(
+        lambda *refs: sum_chunks(*refs, 1 << len(far)),
+        out_shape=shape((packed.shape[0] >> len(near) << len(far), TILE), bf16),
+        in_specs=[VMEM], out_specs=VMEM, compiler_params=small,
+    )(arrived)
+    arrived = exchange(shared, far, owners)
     shared, grad_features = pl.pallas_call(
-        lambda *refs: sum_kernel(owners, *refs),
+        lambda *refs: finish_kernel(1 << len(near), *refs),
         out_shape=[packed, shape(features.shape, bf16)],
-        in_specs=[VMEM, SMEM, SMEM] + [VMEM] * 5,
+        in_specs=[VMEM, HBM, HBM] + [VMEM] * 5,
         out_specs=[VMEM] * 2,
-        scratch_shapes=[pltpu.VMEM((TILE, voxels), bf16)],
-        compiler_params=limit,
-    )(partial, send_slab, send_cross, slab_first, slab_second, cross_first, cross_second, arrived)
-    gathered = lax.all_to_all(shared, ("slab", "cross"), 0, 0, tiled=True)
+        scratch_shapes=[
+            pltpu.VMEM((TILE, voxels), bf16),
+            pltpu.SMEM(send_slab.shape, jnp.int32),
+            pltpu.SMEM(send_cross.shape, jnp.int32),
+            pltpu.SemaphoreType.DMA((2,)),
+        ],
+        compiler_params=small,
+    )(partial, send_slab, send_cross, *returned, arrived)
+    gathered = exchange(shared, near, owners)
     scale = 1.0 / math.sqrt(owners * total)
     kernel_grad, bias_grad = pl.pallas_call(
         lambda *refs: unpack_kernel(scale, *refs),
         out_shape=[shape(weights.shape, f32), shape((1, out_channels), f32)],
         in_specs=[VMEM],
         out_specs=[VMEM] * 2,
-        compiler_params=limit,
+        compiler_params=small,
     )(gathered)
     return grad_features, kernel_grad, bias_grad.reshape(out_channels)
 

time: 103 us -> 82.3 us (0.80)
  starting transfers between devices: 49.4 us -> 35.3 us
  local copies, waits for them, and re-layouts: 5.62 us -> 1.37 us
  blocking collectives: 35.1 us -> 31.2 us
  Pallas kernels: 7.03 us -> 9.62 us
  waiting for transfers between devices: 4.21 us -> 2.7 us
    all_to_all x1, starting transfers between devices: 22.8 us -> 12.5 us  [exchange(): lax.all_to_all(value, ('slab', 'cross'), 0, 0, axis_index_groups=groups_o...]
    unnamed x18 -> x12, local copies, waits for them, and re-layouts: 5.62 us -> 1.37 us
    all_to_all x1 -> x2, blocking collectives: 35.1 us -> 31.2 us  [exchange(): lax.all_to_all(value, ('slab', 'cross'), 0, 0, axis_index_groups=groups_o...]
    ppermute x8, starting transfers between devices: 26.6 us -> 22.9 us  [pairs(): lax.ppermute(value, axis, [pair for low in lows for pair in ((low, low +...]
    pallas_call x2 -> x3, Pallas kernels: 2.54 us -> 4.21 us  [the longest x1 1.95 us: local(): pl.pallas_call(send_kernel, out_shape=[face_pair] * 4, in_specs=[HBM] * 3...]
    all_to_all x1, waiting for transfers between devices: 2.01 us -> 0.88 us  [exchange(): lax.all_to_all(value, ('slab', 'cross'), 0, 0, axis_index_groups=groups_o...]
where the time goes in v2:
time: 82.3 us; the launch traced here: 81.7 us
  starting transfers between devices  35.3 us (43%)
  blocking collectives  31.2 us (38%)
  Pallas kernels  9.62 us (12%)
  waiting for transfers between devices  2.7 us (3%)
  between operations  1.45 us (2%)
  local copies, waits for them, and re-layouts  1.37 us (2%)
    all_to_all x2, blocking collectives, exchange(): lax.all_to_all(value, ('slab', 'cross'), 0, 0, axis_index_groups=groups_o...  31.2 us
    ppermute x8, starting transfers between devices, pairs(): lax.ppermute(value, axis, [pair for low in lows for pair in ((low, low +...  22.9 us
    all_to_all x1, starting transfers between devices, exchange(): lax.all_to_all(value, ('slab', 'cross'), 0, 0, axis_index_groups=groups_o...  12.5 us
    pallas_call x1, Pallas kernels, local(): pl.pallas_call(main_kernel, out_shape=[face_pair] * 4 + [packed, shape((c...  4.45 us
    pallas_call x1, Pallas kernels, local(): pl.pallas_call(send_kernel, out_shape=[face_pair] * 4, in_specs=[HBM] * 3...  1.95 us
    ppermute x8, waiting for transfers between devices, pairs(): lax.ppermute(value, axis, [pair for low in lows for pair in ((low, low +...  1.81 us
  transfers between devices with their start and end apart: 9, of which 3 were waited for; matrix products, arithmetic and copies ran while one was open for 0% of the time, Pallas kernels for 0%

profile of v2, /device:TPU:1, one launch (start us, length us, event | category | flops | bytes accessed | tf_op | source)
XLA Modules:
  0.0 81.7 jit_solution(7583795874634168644)
XLA Ops:
  0.6 0.0 copy-start
  0.6 2.0 %shard_map.103 = (bf16[96,128]{1,0:T(8,128)(2,1)}, bf16[96,128]{1,0:T(8,128)(2,1)}, bf16[96,128]{1,0:T(8,128)(2,1)}, bf16[96,128]{1,0:T(8,128)(2,1)}) custom-call(bf16[1,1,2,96,512]{4,3,2,1,0:T(8,128)(2,1)} %features_in.3, s32[1,1,2,2]{3,2,1,0:T(2,128)} %refs_1_.1, s32[1,1,2,2]{3,2,1,0:T(2,128)} %refs_2_.1), custom_call_target="tpu_custom_call" | custom-call | tf_op jit(solution)/shard_map/pallas_call | solution.py:311
  2.6 0.7 collective-permute-start
  3.3 6.4 %collective-permute-start.1 = (bf16[96,128]{1,0:T(8,128)(2,1)}, bf16[96,128]{1,0:T(8,128)(2,1)S(1)}, u32[]{:S(2)}, u32[]{:S(2)}) collective-permute-start(bf16[96,128]{1,0:T(8,128)(2,1)} %get-tuple-element.18), channel_id=1, source_target_pairs={{0,4},{4,0},{8,12},{12,8},{16,20},{20,16},{24,28},{28,24},{32,36},... | collective-permute-start | bytes 73736 | tf_op jit(solution)/shard_map/ppermute | solution.py:286
  9.7 4.3 %collective-permute-start.2 = (bf16[96,128]{1,0:T(8,128)(2,1)}, bf16[96,128]{1,0:T(8,128)(2,1)S(1)}, u32[]{:S(2)}, u32[]{:S(2)}) collective-permute-start(bf16[96,128]{1,0:T(8,128)(2,1)} %get-tuple-element.19), channel_id=1, source_target_pairs={{1,2},{2,1},{5,6},{6,5},{9,10},{10,9},{13,14},{14,13},{17,18},{18,... | collective-permute-start | bytes 73736 | tf_op jit(solution)/shard_map/ppermute | solution.py:286
  14.0 1.9 %collective-permute-start.3 = (bf16[96,128]{1,0:T(8,128)(2,1)}, bf16[96,128]{1,0:T(8,128)(2,1)S(1)}, u32[]{:S(2)}, u32[]{:S(2)}) collective-permute-start(bf16[96,128]{1,0:T(8,128)(2,1)} %get-tuple-element.20), channel_id=1, source_target_pairs={{0,1},{1,0},{2,3},{3,2},{4,5},{5,4},{6,7},{7,6},{8,9},{9,8},{10,11... | collective-permute-start | bytes 73736 | tf_op jit(solution)/shard_map/ppermute | solution.py:286
  15.9 0.0 copy-start.5
  16.6 0.0 collective-permute-done.refs_0_
  16.6 0.0 collective-permute-done.1.refs_1_
  16.6 0.0 collective-permute-done.2.refs_2_
  16.6 0.7 collective-permute-done.3.refs_3_
  17.3 0.0 copy-start.4
  17.3 0.0 copy-done
  17.3 0.0 copy-done.5
  17.3 0.7 copy-done.4
  18.0 4.4 %shard_map.104 = (bf16[96,128]{1,0:T(8,128)(2,1)S(1)}, bf16[96,128]{1,0:T(8,128)(2,1)S(1)}, bf16[96,128]{1,0:T(8,128)(2,1)S(1)}, bf16[96,128]{1,0:T(8,128)(2,1)S...) custom-call(bf16[1,1,2,96,512]{4,3,2,1,0:T(8,128)(2,1)S(1)} %copy-done, bf16[672,192]{1,0:T(8,128)(2,1)} %bitcast.14, ...), custom_call_target="tpu_custom_call" | custom-call | tf_op jit(solution)/shard_map/pallas_call | solution.py:325
  22.5 15.5 %all_to_all.33 = bf16[32,32,128]{2,1,0:T(8,128)(2,1)S(1)} all-to-all(bf16[32,32,128]{2,1,0:T(8,128)(2,1)} %bitcast.15), channel_id=1, replica_groups={{0,1,2,3,4,5,6,7,8,9,10,11,12,13,14,15,64,65,66,67,68,69,70,71,72,73,74..., dimensions={0} | all-to-all | bytes 524288 | tf_op jit(solution)/shard_map/all_to_all | solution.py:293
  37.9 0.0 copy-start.1
  37.9 0.7 shard_map.105
  38.6 0.0 copy-start.3
  38.6 12.5 %all-to-all-start.1 = ((bf16[16,32,128]{2,1,0:T(8,128)(2,1)}), bf16[16,32,128]{2,1,0:T(8,128)(2,1)S(1)}, u32[]{:S(2)}, u32[]{:S(2)}) async-start(bf16[16,32,128]{2,1,0:T(8,128)(2,1)} %bitcast.4), calls=%async_computation.1 | async-start | bytes 262144 | tf_op jit(solution)/shard_map/all_to_all | solution.py:293
  51.1 0.7 collective-permute-start.4
  51.8 3.1 %collective-permute-start.5 = (bf16[96,128]{1,0:T(8,128)(2,1)S(1)}, bf16[96,128]{1,0:T(8,128)(2,1)S(1)}, u32[]{:S(2)}, u32[]{:S(2)}) collective-permute-start(bf16[96,128]{1,0:T(8,128)(2,1)S(1)} %get-tuple-element.23), channel_id=1, source_target_pairs={{0,4},{4,0},{8,12},{12,8},{16,20},{20,16},{24,28},{28,24},{32,36},... | collective-permute-start | bytes 73736 | tf_op jit(solution)/shard_map/ppermute | solution.py:286
  54.9 3.8 %collective-permute-start.6 = (bf16[96,128]{1,0:T(8,128)(2,1)S(1)}, bf16[96,128]{1,0:T(8,128)(2,1)S(1)}, u32[]{:S(2)}, u32[]{:S(2)}) collective-permute-start(bf16[96,128]{1,0:T(8,128)(2,1)S(1)} %get-tuple-element.24), channel_id=1, source_target_pairs={{1,2},{2,1},{5,6},{6,5},{9,10},{10,9},{13,14},{14,13},{17,18},{18,... | collective-permute-start | bytes 73736 | tf_op jit(solution)/shard_map/ppermute | solution.py:286
  58.8 1.9 %collective-permute-start.7 = (bf16[96,128]{1,0:T(8,128)(2,1)S(1)}, bf16[96,128]{1,0:T(8,128)(2,1)S(1)}, u32[]{:S(2)}, u32[]{:S(2)}) collective-permute-start(bf16[96,128]{1,0:T(8,128)(2,1)S(1)} %get-tuple-element.25), channel_id=1, source_target_pairs={{0,1},{1,0},{2,3},{3,2},{4,5},{5,4},{6,7},{7,6},{8,9},{9,8},{10,11... | collective-permute-start | bytes 73736 | tf_op jit(solution)/shard_map/ppermute | solution.py:286
  60.7 0.0 collective-permute-done.4.refs_3_
  60.7 0.0 collective-permute-done.5.refs_4_
  60.7 0.0 collective-permute-done.6.refs_5_
  60.7 1.1 %collective-permute-done.7.refs_6_ = bf16[96,128]{1,0:T(8,128)(2,1)S(1)} collective-permute-done((bf16[96,128]{1,0:T(8,128)(2,1)S(1)}, bf16[96,128]{1,0:T(8,128)(2,1)S(1)}, u32[]{:S(2)}, u32[]{:S(2)}) %collective-permute-start.7) | collective-permute-done | bytes 24608 | tf_op jit(solution)/shard_map/ppermute | solution.py:286
  61.9 0.9 %all-to-all-done.1 = bf16[16,32,128]{2,1,0:T(8,128)(2,1)S(1)} async-done(((bf16[16,32,128]{2,1,0:T(8,128)(2,1)}), bf16[16,32,128]{2,1,0:T(8,128)(2,1)S(1)}, u32[]{:S(2)}, u32[]{:S(2)}) %all-to-all-start.1) | async-done | bytes 131104 | tf_op jit(solution)/shard_map/all_to_all | solution.py:293
  62.7 0.0 copy-start.2
  62.7 0.0 copy-done.1
  62.8 0.0 copy-done.3
  62.8 0.7 copy-done.2
  63.4 1.6 %shard_map.106 = (bf16[1024,128]{1,0:T(8,128)(2,1)S(1)}, bf16[1,1,2,96,512]{4,3,2,1,0:T(8,128)(2,1)}) custom-call(f32[96,1024]{1,0:T(8,128)S(1)} %copy-done.1, s32[1,1,2,2]{3,2,1,0:T(2,128)S(1)} %copy-done.2, s32[1,1,2,2]{3,2,1,0:T(2,128)S(1)} %copy-done.3, bf16[96,128]{1,0:T(8,128)(2,1)S(1)} %collective-permute-done.4.refs_3_, ...), custom_call_target="tpu_custom_call" | custom-call | tf_op jit(solution)/shard_map/pallas_call | solution.py:359
  65.0 15.8 %all_to_all.34 = bf16[32,32,128]{2,1,0:T(8,128)(2,1)S(1)} all-to-all(bf16[32,32,128]{2,1,0:T(8,128)(2,1)S(1)} %bitcast.12), channel_id=1, replica_groups={{0,1,2,3,4,5,6,7,8,9,10,11,12,13,14,15,64,65,66,67,68,69,70,71,72,73,74..., dimensions={0} | all-to-all | bytes 524288 | tf_op jit(solution)/shard_map/all_to_all | solution.py:293
  80.7 1.0 %shard_map.107 = (f32[7,96,192]{2,1,0:T(8,128)}, f32[1,192]{1,0:T(1,128)}) custom-call(bf16[1024,128]{1,0:T(8,128)(2,1)S(1)} %bitcast.9), custom_call_target="tpu_custom_call" | custom-call | tf_op jit(solution)/shard_map/pallas_call | solution.py:374
Async XLA Ops:
  0.6 16.7 %copy-start = (bf16[1,1,2,96,512]{4,3,2,1,0:T(8,128)(2,1)S(1)}, bf16[1,1,2,96,512]{4,3,2,1,0:T(8,128)(2,1)}, u32[]{:S(2)}) copy-start(bf16[1,1,2,96,512]{4,3,2,1,0:T(8,128)(2,1)} %features_in.3) | copy-start | bytes 589828
  2.6 14.0 %collective-permute-start = (bf16[96,128]{1,0:T(8,128)(2,1)}, bf16[96,128]{1,0:T(8,128)(2,1)S(1)}, u32[]{:S(2)}, u32[]{:S(2)}) collective-permute-start(bf16[96,128]{1,0:T(8,128)(2,1)} %get-tuple-element.17), channel_id=1, source_target_pairs={{4,8},{8,4},{12,16},{16,12},{20,24},{24,20},{28,32},{32,28},{36,40... | collective-permute-start | bytes 73736 | tf_op jit(solution)/shard_map/ppermute | solution.py:286
  3.3 13.4 %collective-permute-start.1 = (bf16[96,128]{1,0:T(8,128)(2,1)}, bf16[96,128]{1,0:T(8,128)(2,1)S(1)}, u32[]{:S(2)}, u32[]{:S(2)}) collective-permute-start(bf16[96,128]{1,0:T(8,128)(2,1)} %get-tuple-element.18), channel_id=1, source_target_pairs={{0,4},{4,0},{8,12},{12,8},{16,20},{20,16},{24,28},{28,24},{32,36},... | collective-permute-start | bytes 73736 | tf_op jit(solution)/shard_map/ppermute | solution.py:286
  9.7 7.0 %collective-permute-start.2 = (bf16[96,128]{1,0:T(8,128)(2,1)}, bf16[96,128]{1,0:T(8,128)(2,1)S(1)}, u32[]{:S(2)}, u32[]{:S(2)}) collective-permute-start(bf16[96,128]{1,0:T(8,128)(2,1)} %get-tuple-element.19), channel_id=1, source_target_pairs={{1,2},{2,1},{5,6},{6,5},{9,10},{10,9},{13,14},{14,13},{17,18},{18,... | collective-permute-start | bytes 73736 | tf_op jit(solution)/shard_map/ppermute | solution.py:286
  14.0 3.3 %collective-permute-start.3 = (bf16[96,128]{1,0:T(8,128)(2,1)}, bf16[96,128]{1,0:T(8,128)(2,1)S(1)}, u32[]{:S(2)}, u32[]{:S(2)}) collective-permute-start(bf16[96,128]{1,0:T(8,128)(2,1)} %get-tuple-element.20), channel_id=1, source_target_pairs={{0,1},{1,0},{2,3},{3,2},{4,5},{5,4},{6,7},{7,6},{8,9},{9,8},{10,11... | collective-permute-start | bytes 73736 | tf_op jit(solution)/shard_map/ppermute | solution.py:286
  15.9 1.4 %copy-start.5 = (s32[1,1,2,6]{3,2,1,0:T(2,128)S(1)}, s32[1,1,2,6]{3,2,1,0:T(2,128)}, u32[]{:S(2)}) copy-start(s32[1,1,2,6]{3,2,1,0:T(2,128)} %links_in.1) | copy-start | bytes 148
  17.3 0.7 copy-start.4
  37.9 24.8 %copy-start.1 = (f32[96,1024]{1,0:T(8,128)S(1)}, f32[96,1024]{1,0:T(8,128)}, u32[]{:S(2)}) copy-start(f32[96,1024]{1,0:T(8,128)} %get-tuple-element.21.refs_0_) | copy-start | bytes 1179652
  38.6 24.1 %copy-start.3 = (s32[1,1,2,2]{3,2,1,0:T(2,128)S(1)}, s32[1,1,2,2]{3,2,1,0:T(2,128)}, u32[]{:S(2)}) copy-start(s32[1,1,2,2]{3,2,1,0:T(2,128)} %refs_2_.1) | copy-start | bytes 52
  38.6 24.1 %all-to-all-start.1 = ((bf16[16,32,128]{2,1,0:T(8,128)(2,1)}), bf16[16,32,128]{2,1,0:T(8,128)(2,1)S(1)}, u32[]{:S(2)}, u32[]{:S(2)}) async-start(bf16[16,32,128]{2,1,0:T(8,128)(2,1)} %bitcast.4), calls=%async_computation.1 | async-start | bytes 262144 | tf_op jit(solution)/shard_map/all_to_all | solution.py:293
  51.1 9.6 %collective-permute-start.4 = (bf16[96,128]{1,0:T(8,128)(2,1)S(1)}, bf16[96,128]{1,0:T(8,128)(2,1)S(1)}, u32[]{:S(2)}, u32[]{:S(2)}) collective-permute-start(bf16[96,128]{1,0:T(8,128)(2,1)S(1)} %get-tuple-element.22), channel_id=1, source_target_pairs={{4,8},{8,4},{12,16},{16,12},{20,24},{24,20},{28,32},{32,28},{36,40... | collective-permute-start | bytes 73736 | tf_op jit(solution)/shard_map/ppermute | solution.py:286
  51.8 8.9 %collective-permute-start.5 = (bf16[96,128]{1,0:T(8,128)(2,1)S(1)}, bf16[96,128]{1,0:T(8,128)(2,1)S(1)}, u32[]{:S(2)}, u32[]{:S(2)}) collective-permute-start(bf16[96,128]{1,0:T(8,128)(2,1)S(1)} %get-tuple-element.23), channel_id=1, source_target_pairs={{0,4},{4,0},{8,12},{12,8},{16,20},{20,16},{24,28},{28,24},{32,36},... | collective-permute-start | bytes 73736 | tf_op jit(solution)/shard_map/ppermute | solution.py:286
  54.9 5.8 %collective-permute-start.6 = (bf16[96,128]{1,0:T(8,128)(2,1)S(1)}, bf16[96,128]{1,0:T(8,128)(2,1)S(1)}, u32[]{:S(2)}, u32[]{:S(2)}) collective-permute-start(bf16[96,128]{1,0:T(8,128)(2,1)S(1)} %get-tuple-element.24), channel_id=1, source_target_pairs={{1,2},{2,1},{5,6},{6,5},{9,10},{10,9},{13,14},{14,13},{17,18},{18,... | collective-permute-start | bytes 73736 | tf_op jit(solution)/shard_map/ppermute | solution.py:286
  58.8 3.1 %collective-permute-start.7 = (bf16[96,128]{1,0:T(8,128)(2,1)S(1)}, bf16[96,128]{1,0:T(8,128)(2,1)S(1)}, u32[]{:S(2)}, u32[]{:S(2)}) collective-permute-start(bf16[96,128]{1,0:T(8,128)(2,1)S(1)} %get-tuple-element.25), channel_id=1, source_target_pairs={{0,1},{1,0},{2,3},{3,2},{4,5},{5,4},{6,7},{7,6},{8,9},{9,8},{10,11... | collective-permute-start | bytes 73736 | tf_op jit(solution)/shard_map/ppermute | solution.py:286
  62.7 0.7 copy-start.2

commit v3 on v2

--- a/solution.py
+++ b/solution.py
@@ -12,13 +12,14 @@
 TILE = 2 * LAYER
 PACK = 16
 FIRST = 60 * 2**20
-MIDDLE = 56_000_000
+MIDDLE = 55_700_000
 NEAR = (0, 1, 2, 3, 6)
 f32 = jnp.float32
 bf16 = jnp.bfloat16
 VMEM = pl.BlockSpec(memory_space=pltpu.VMEM)
 SMEM = pl.BlockSpec(memory_space=pltpu.SMEM)
 HBM = pl.BlockSpec(memory_space=pltpu.HBM)
+ANY = pl.BlockSpec(memory_space=pl.ANY)
 
 
 def nn(a, b):
@@ -109,8 +110,8 @@
 
 
 def main_kernel(features_in, weights_in, upstream_in, bias_in, count_in, links_in, *refs):
-    received, sent, (terms, partial), refs = refs[:4], refs[4:8], refs[8:10], refs[10:]
-    features, weights, upstream, bias, count, links, fields, grad, taps, table, marks, table_grad, arrivals = refs
+    received, (terms, grad), refs = refs[:4], refs[4:6], refs[6:]
+    features, weights, upstream, bias, count, links, fields, taps, table, marks, arrivals = refs
     copies = fetch(
         (features_in, links_in, weights_in, bias_in, count_in, upstream_in),
         (features, links, weights, bias, count, upstream), arrivals)
@@ -188,7 +189,23 @@
     terms[depth + middle:] = jnp.where(row == 0, found[depth:, :TILE],
                                        jnp.where(row == 1, found[depth:, TILE:], 0.0)).astype(bf16)
 
+
+def back_kernel(weights, grad, links_in, *refs):
+    sent, (partial, marks, table_grad, links, arrivals) = refs[:4], refs[4:]
+    copies = fetch((links_in,), (links,), arrivals)
+    channels, total = partial.shape
+    number = links.shape[2]
+    voxels = total // number
+    out_channels = weights.shape[1]
+    own = 6 * number
+    half = low_half(channels)
+    v = lax.broadcasted_iota(jnp.int32, (channels, total), 1) & (voxels - 1)
+    coords = (v >> 6, (v >> 3) & 7, v & 7)
+    strides = (LAYER, EDGE, 1)
+    for axis in (1, 2):
+        marks[TILE * (axis - 1):TILE * axis] = layer_map(axis, voxels)
     table_grad[...] = jnp.zeros(table_grad.shape, f32)
+    copies[0].wait()
     live = grad[:out_channels]
     summed = nn(weights[:channels], live)
     for axis in range(3):
@@ -232,9 +249,9 @@
     shared[...] = jnp.broadcast_to(value[None], (parts, rows, TILE)).reshape(shared.shape)
 
 
-def finish_kernel(parts, partial, slab_in, cross_in, slab_far, slab_near, cross_far, cross_near, arrived, shared, result, marks, slab_list, cross_list, arrivals):
+def finish_kernel(partial, slab_in, cross_in, slab_far, slab_near, cross_far, cross_near, result, marks, slab_list,
+                  cross_list, arrivals):
     copies = fetch((slab_in, cross_in), (slab_list, cross_list), arrivals)
-    sum_chunks(arrived, shared, parts)
     number, channels, voxels = result.shape[2:]
     half = low_half(channels)
     marks[...] = layer_map(1, voxels)
@@ -280,13 +297,24 @@
     return list(found.values())
 
 
-def swap(slab_far, slab_near, cross_far, cross_near):
-    def pairs(value, axis, first):
+def swap(far, near, axis):
+    def pairs(value, first):
         lows = range(first, lax.axis_size(axis) - 1, 2)
         return lax.ppermute(value, axis, [pair for low in lows for pair in ((low, low + 1), (low + 1, low))])
 
-    return (pairs(slab_far, "slab", 1), pairs(slab_near, "slab", 0),
-            pairs(cross_far, "cross", 1), pairs(cross_near, "cross", 0))
+    return pairs(far, 1), pairs(near, 0)
+
+
+def staged_sum(arrived, rows, parts, ended, passed, params):
+    shared, *passed = pl.pallas_call(
+        lambda arrived, *refs: sum_chunks(arrived, refs[len(ended) + len(passed)], parts),
+        out_shape=[shape((rows, TILE), bf16)] + [shape(x.shape, x.dtype) for x in passed],
+        in_specs=[VMEM] + [ANY] * (len(ended) + len(passed)),
+        out_specs=[VMEM] + [ANY] * len(passed),
+        input_output_aliases={1 + len(ended) + k: 1 + k for k in range(len(passed))},
+        compiler_params=params,
+    )(arrived, *ended, *passed)
+    return shared, passed
 
 
 def exchange(value, bits, count):
@@ -322,11 +350,11 @@
         compiler_params=limit,
     )(features, send_slab, send_cross)
     packed = shape((depth * 3 // 2 + PACK, TILE), bf16)
-    *backs, terms, partial = pl.pallas_call(
+    terms, grad = pl.pallas_call(
         main_kernel,
-        out_shape=[face_pair] * 4 + [packed, shape((channels, total), f32)],
+        out_shape=[packed, shape((2 * TILE, total), bf16)],
         in_specs=[HBM] * 6 + [VMEM] * 4,
-        out_specs=[VMEM] * 6,
+        out_specs=[VMEM] * 2,
         scratch_shapes=[
             pltpu.VMEM(features.shape, bf16),
             pltpu.VMEM((depth, out_channels), bf16),
@@ -335,32 +363,43 @@
             pltpu.SMEM(brick_count.shape, jnp.int32),
             pltpu.SMEM(neighbours.shape, jnp.int32),
             pltpu.VMEM((depth + PACK, total), bf16),
-            pltpu.VMEM((2 * TILE, total), bf16),
             pltpu.VMEM((depth + PACK, out_channels), bf16),
             pltpu.VMEM((6 * number + 9, channels, TILE), f32),
             pltpu.VMEM((2 * TILE, voxels), bf16),
-            pltpu.VMEM((6 * number + 9, channels, TILE), f32),
             pltpu.SemaphoreType.DMA((6,)),
         ],
         compiler_params=middle,
     )(features, weights.reshape(depth, out_channels), out_grad, conv_bias.reshape(1, out_channels), brick_count,
-      neighbours, *swap(*sends))
-    returned = swap(*backs)
+      neighbours, *swap(*sends[:2], "slab"), *swap(*sends[2:], "cross"))
+    *backs, partial = pl.pallas_call(
+        back_kernel,
+        out_shape=[face_pair] * 4 + [shape((channels, total), f32)],
+        in_specs=[VMEM, VMEM, HBM],
+        out_specs=[VMEM] * 5,
+        scratch_shapes=[
+            pltpu.VMEM((2 * TILE, voxels), bf16),
+            pltpu.VMEM((6 * number + 9, channels, TILE), f32),
+            pltpu.SMEM(neighbours.shape, jnp.int32),
+            pltpu.SemaphoreType.DMA((1,)),
+        ],
+        compiler_params=small,
+    )(weights.reshape(depth, out_channels), grad, neighbours)
 
     near = NEAR if owners == 512 else tuple(range(owners.bit_length() // 2))
     far = tuple(bit for bit in range(owners.bit_length() - 1) if bit not in near)
     arrived = exchange(terms, near, owners)
-    shared = pl.pallas_call(
-        lambda *refs: sum_chunks(*refs, 1 << len(far)),
-        out_shape=shape((packed.shape[0] >> len(near) << len(far), TILE), bf16),
-        in_specs=[VMEM], out_specs=VMEM, compiler_params=small,
-    )(arrived)
+    shared, slab_back = staged_sum(
+        arrived, packed.shape[0] >> len(near) << len(far), 1 << len(far), [], backs[:2], small)
     arrived = exchange(shared, far, owners)
-    shared, grad_features = pl.pallas_call(
-        lambda *refs: finish_kernel(1 << len(near), *refs),
-        out_shape=[packed, shape(features.shape, bf16)],
-        in_specs=[VMEM, HBM, HBM] + [VMEM] * 5,
-        out_specs=[VMEM] * 2,
+    slab_back = swap(*slab_back, "slab")
+    shared, passed = staged_sum(
+        arrived, packed.shape[0], 1 << len(near), slab_back, [partial, *backs[2:]], small)
+    partial, cross_back = passed[0], swap(*passed[1:], "cross")
+    grad_features = pl.pallas_call(
+        finish_kernel,
+        out_shape=shape(features.shape, bf16),
+        in_specs=[VMEM, HBM, HBM] + [VMEM] * 4,
+        out_specs=VMEM,
         scratch_shapes=[
             pltpu.VMEM((TILE, voxels), bf16),
             pltpu.SMEM(send_slab.shape, jnp.int32),
@@ -368,7 +407,7 @@
             pltpu.SemaphoreType.DMA((2,)),
         ],
         compiler_params=small,
-    )(partial, send_slab, send_cross, *returned, arrived)
+    )(partial, send_slab, send_cross, *slab_back, *cross_back)
     gathered = exchange(shared, near, owners)
     scale = 1.0 / math.sqrt(owners * total)
     kernel_grad, bias_grad = pl.pallas_call(

time: 82.3 us -> 77.1 us (0.937)
  blocking collectives: 31.2 us -> 0 us
  waiting for transfers between devices: 2.7 us -> 15.1 us
  starting transfers between devices: 35.3 us -> 47 us
  Pallas kernels: 9.62 us -> 11.1 us
    all_to_all x2 -> x0, blocking collectives: 31.2 us -> none  [exchange(): lax.all_to_all(value, ('slab', 'cross'), 0, 0, axis_index_groups=groups_o...]
    all_to_all x1 -> x3, starting transfers between devices: 12.5 us -> 24.4 us  [exchange(): lax.all_to_all(value, ('slab', 'cross'), 0, 0, axis_index_groups=groups_o...]
    all_to_all x1 -> x3, waiting for transfers between devices: 0.88 us -> 11.6 us  [exchange(): lax.all_to_all(value, ('slab', 'cross'), 0, 0, axis_index_groups=groups_o...]
    ppermute x8, waiting for transfers between devices: 1.81 us -> 3.54 us  [pairs(): lax.ppermute(value, axis, [pair for low in lows for pair in ((low, low +...]
    pallas_call x3 -> x5, Pallas kernels: 6.7 us -> 8.18 us  [the longest x1 3.27 us: local(): pl.pallas_call(main_kernel, out_shape=[packed, shape((2 * TILE, total), b...]
    unnamed x12 -> x14, local copies, waits for them, and re-layouts: 1.37 us -> 1.74 us
  transfers between devices with their start and end apart: 9 -> 11, of which waited for: 3 -> 7; matrix products, arithmetic and copies ran while one was open for 0% -> 0% of each run, Pallas kernels for 0% -> 5%
where the time goes in v3:
time: 77.1 us; the launch traced here: 76.4 us
  starting transfers between devices  47 us (61%)
  waiting for transfers between devices  15.1 us (20%)
  Pallas kernels  11.1 us (14%)
  local copies, waits for them, and re-layouts  1.74 us (2%)
  between operations  1.5 us (2%)
    all_to_all x3, starting transfers between devices, exchange(): lax.all_to_all(value, ('slab', 'cross'), 0, 0, axis_index_groups=groups_o...  24.4 us
    ppermute x8, starting transfers between devices, pairs(): lax.ppermute(value, axis, [pair for low in lows for pair in ((low, low +...  22.6 us
    all_to_all x3, waiting for transfers between devices, exchange(): lax.all_to_all(value, ('slab', 'cross'), 0, 0, axis_index_groups=groups_o...  11.6 us
    ppermute x8, waiting for transfers between devices, pairs(): lax.ppermute(value, axis, [pair for low in lows for pair in ((low, low +...  3.54 us
    pallas_call x1, Pallas kernels, local(): pl.pallas_call(main_kernel, out_shape=[packed, shape((2 * TILE, total), b...  3.27 us
    pallas_call x1, Pallas kernels, local(): pl.pallas_call(send_kernel, out_shape=[face_pair] * 4, in_specs=[HBM] * 3...  1.96 us
    pallas_call x1, Pallas kernels, local(): pl.pallas_call(back_kernel, out_shape=[face_pair] * 4 + [shape((channels,...  1.91 us
    unnamed x14, local copies, waits for them, and re-layouts  1.74 us
  transfers between devices with their start and end apart: 11, of which 7 were waited for; matrix products, arithmetic and copies ran while one was open for 0% of the time, Pallas kernels for 5%

profile of v3, /device:TPU:1, one launch (start us, length us, event | category | flops | bytes accessed | tf_op | source)
XLA Modules:
  0.0 76.4 jit_solution(8723312719702202858)
XLA Ops:
  0.6 0.0 copy-start.1
  0.6 2.0 %shard_map.103 = (bf16[96,128]{1,0:T(8,128)(2,1)}, bf16[96,128]{1,0:T(8,128)(2,1)}, bf16[96,128]{1,0:T(8,128)(2,1)}, bf16[96,128]{1,0:T(8,128)(2,1)}) custom-call(bf16[1,1,2,96,512]{4,3,2,1,0:T(8,128)(2,1)} %features_in.3, s32[1,1,2,2]{3,2,1,0:T(2,128)} %slab_in.3, s32[1,1,2,2]{3,2,1,0:T(2,128)} %cross_in.3), custom_call_target="tpu_custom_call" | custom-call | tf_op jit(solution)/shard_map/pallas_call | solution.py:339
  2.6 0.7 collective-permute-start
  3.3 6.4 %collective-permute-start.1 = (bf16[96,128]{1,0:T(8,128)(2,1)}, bf16[96,128]{1,0:T(8,128)(2,1)S(1)}, u32[]{:S(2)}, u32[]{:S(2)}) collective-permute-start(bf16[96,128]{1,0:T(8,128)(2,1)} %get-tuple-element.24), channel_id=1, source_target_pairs={{0,4},{4,0},{8,12},{12,8},{16,20},{20,16},{24,28},{28,24},{32,36},... | collective-permute-start | bytes 73736 | tf_op jit(solution)/shard_map/ppermute | solution.py:303
  9.7 4.3 %collective-permute-start.2 = (bf16[96,128]{1,0:T(8,128)(2,1)}, bf16[96,128]{1,0:T(8,128)(2,1)S(1)}, u32[]{:S(2)}, u32[]{:S(2)}) collective-permute-start(bf16[96,128]{1,0:T(8,128)(2,1)} %get-tuple-element.25), channel_id=1, source_target_pairs={{1,2},{2,1},{5,6},{6,5},{9,10},{10,9},{13,14},{14,13},{17,18},{18,... | collective-permute-start | bytes 73736 | tf_op jit(solution)/shard_map/ppermute | solution.py:303
  14.0 1.9 %collective-permute-start.3 = (bf16[96,128]{1,0:T(8,128)(2,1)}, bf16[96,128]{1,0:T(8,128)(2,1)S(1)}, u32[]{:S(2)}, u32[]{:S(2)}) collective-permute-start(bf16[96,128]{1,0:T(8,128)(2,1)} %get-tuple-element.26), channel_id=1, source_target_pairs={{0,1},{1,0},{2,3},{3,2},{4,5},{5,4},{6,7},{7,6},{8,9},{9,8},{10,11... | collective-permute-start | bytes 73736 | tf_op jit(solution)/shard_map/ppermute | solution.py:303
  15.9 0.0 copy-start.6
  16.6 0.0 collective-permute-done.refs_0_
  16.6 0.0 collective-permute-done.1.refs_1_
  16.6 0.0 collective-permute-done.2.refs_2_
  16.6 0.7 collective-permute-done.3.refs_3_
  17.3 0.0 copy-start.3
  17.3 0.0 copy-done.1
  17.3 0.0 copy-done.6
  17.3 0.7 copy-done.3
  18.0 3.3 %shard_map.104 = (bf16[1024,128]{1,0:T(8,128)(2,1)}, bf16[256,1024]{1,0:T(8,128)(2,1)}) custom-call(bf16[1,1,2,96,512]{4,3,2,1,0:T(8,128)(2,1)S(1)} %copy-done.1, bf16[672,192]{1,0:T(8,128)(2,1)} %bitcast.9, bf16[1,1,2,192,512]{4,3,2,1,0:T(8,128)(2,1)} %upstream_in.1, f32[1,192]{1,0:T(1,128)S(1)} %bitcast.14, s32[1,1]{1,0:T(1,128)S(6)} %copy.21.count_in, ...), custom_call_target="tpu_custom_call" | custom-call | tf_op jit(solution)/shard_map/pallas_call | solution.py:353
  21.3 0.0 copy-start
  21.3 7.3 %all-to-all-start = ((bf16[32,32,128]{2,1,0:T(8,128)(2,1)}), bf16[32,32,128]{2,1,0:T(8,128)(2,1)S(1)}, u32[]{:S(2)}, u32[]{:S(2)}) async-start(bf16[32,32,128]{2,1,0:T(8,128)(2,1)} %bitcast.2), calls=%async_computation | async-start | bytes 524288 | tf_op jit(solution)/shard_map/all_to_all | solution.py:321
  28.6 0.0 copy-done
  28.6 0.0 copy-start.2
  28.6 1.0 %copy-done.2 = bf16[256,1024]{1,0:T(8,128)(2,1)S(1)} copy-done((bf16[256,1024]{1,0:T(8,128)(2,1)S(1)}, bf16[256,1024]{1,0:T(8,128)(2,1)}, u32[]{:S(2)}) %copy-start.2) | copy-done | bytes 524312
  29.6 1.9 %shard_map.105 = (bf16[96,128]{1,0:T(8,128)(2,1)S(1)}, bf16[96,128]{1,0:T(8,128)(2,1)S(1)}, bf16[96,128]{1,0:T(8,128)(2,1)S(1)}, bf16[96,128]{1,0:T(8,128)(2,1)S(1)}, f32[96,1024]{1,0:T(8,128)S(1)}) custom-call(bf16[672,192]{1,0:T(8,128)(2,1)S(1)} %bitcast.10, bf16[256,1024]{1,0:T(8,128)(2,1)S(1)} %copy-done.2, s32[1,1,2,6]{3,2,1,0:T(2,128)S(1)} %copy-done.3), custom_call_target="tpu_custom_call" | custom-call | tf_op jit(solution)/shard_map/pallas_call | solution.py:374
  31.6 5.4 %all-to-all-done = bf16[32,32,128]{2,1,0:T(8,128)(2,1)S(1)} async-done(((bf16[32,32,128]{2,1,0:T(8,128)(2,1)}), bf16[32,32,128]{2,1,0:T(8,128)(2,1)S(1)}, u32[]{:S(2)}, u32[]{:S(2)}) %all-to-all-start) | async-done | bytes 262176 | tf_op jit(solution)/shard_map/all_to_all | solution.py:321
  36.9 0.7 shard_map.106
  37.6 12.3 %all-to-all-start.1 = ((bf16[16,32,128]{2,1,0:T(8,128)(2,1)}), bf16[16,32,128]{2,1,0:T(8,128)(2,1)S(1)}, u32[]{:S(2)}, u32[]{:S(2)}) async-start(bf16[16,32,128]{2,1,0:T(8,128)(2,1)} %bitcast.4), calls=%async_computation.1 | async-start | bytes 262144 | tf_op jit(solution)/shard_map/all_to_all | solution.py:321
  49.9 0.7 collective-permute-start.4
  50.6 3.1 %collective-permute-start.5 = (bf16[96,128]{1,0:T(8,128)(2,1)S(1)}, bf16[96,128]{1,0:T(8,128)(2,1)S(1)}, u32[]{:S(2)}, u32[]{:S(2)}) collective-permute-start(bf16[96,128]{1,0:T(8,128)(2,1)S(1)} %get-tuple-element.33), channel_id=1, source_target_pairs={{0,4},{4,0},{8,12},{12,8},{16,20},{20,16},{24,28},{28,24},{32,36},... | collective-permute-start | bytes 73736 | tf_op jit(solution)/shard_map/ppermute | solution.py:303
  53.8 0.0 collective-permute-done.4.refs_0_.slab_far
  53.8 1.7 %collective-permute-done.5.refs_1_.slab_near = bf16[96,128]{1,0:T(8,128)(2,1)S(1)} collective-permute-done((bf16[96,128]{1,0:T(8,128)(2,1)S(1)}, bf16[96,128]{1,0:T(8,128)(2,1)S(1)}, u32[]{:S(2)}, u32[]{:S(2)}) %collective-permute-start.5) | collective-permute-done | bytes 24608 | tf_op jit(solution)/shard_map/ppermute | solution.py:303
  55.5 6.1 %all-to-all-done.1 = bf16[16,32,128]{2,1,0:T(8,128)(2,1)S(1)} async-done(((bf16[16,32,128]{2,1,0:T(8,128)(2,1)}), bf16[16,32,128]{2,1,0:T(8,128)(2,1)S(1)}, u32[]{:S(2)}, u32[]{:S(2)}) %all-to-all-start.1) | async-done | bytes 131104 | tf_op jit(solution)/shard_map/all_to_all | solution.py:321
  61.6 0.7 shard_map.107
  62.3 4.8 %all-to-all-start.2 = ((bf16[32,32,128]{2,1,0:T(8,128)(2,1)}), bf16[32,32,128]{2,1,0:T(8,128)(2,1)S(1)}, u32[]{:S(2)}, u32[]{:S(2)}) async-start(bf16[32,32,128]{2,1,0:T(8,128)(2,1)} %bitcast.6), calls=%async_computation.2 | async-start | bytes 524288 | tf_op jit(solution)/shard_map/all_to_all | solution.py:321
  67.1 3.5 %collective-permute-start.6 = (bf16[96,128]{1,0:T(8,128)(2,1)S(1)}, bf16[96,128]{1,0:T(8,128)(2,1)S(1)}, u32[]{:S(2)}, u32[]{:S(2)}) collective-permute-start(bf16[96,128]{1,0:T(8,128)(2,1)S(1)} %get-tuple-element.38), channel_id=1, source_target_pairs={{1,2},{2,1},{5,6},{6,5},{9,10},{10,9},{13,14},{14,13},{17,18},{18,... | collective-permute-start | bytes 73736 | tf_op jit(solution)/shard_map/ppermute | solution.py:303
  70.7 0.0 copy-start.5
  70.7 0.0 copy-start.4
  70.7 1.9 %collective-permute-start.7 = (bf16[96,128]{1,0:T(8,128)(2,1)S(1)}, bf16[96,128]{1,0:T(8,128)(2,1)S(1)}, u32[]{:S(2)}, u32[]{:S(2)}) collective-permute-start(bf16[96,128]{1,0:T(8,128)(2,1)S(1)} %get-tuple-element.39), channel_id=1, source_target_pairs={{0,1},{1,0},{2,3},{3,2},{4,5},{5,4},{6,7},{7,6},{8,9},{9,8},{10,11... | collective-permute-start | bytes 73736 | tf_op jit(solution)/shard_map/ppermute | solution.py:303
  72.6 0.3 collective-permute-done.6.cross_far
  72.9 0.9 %collective-permute-done.7.cross_near = bf16[96,128]{1,0:T(8,128)(2,1)S(1)} collective-permute-done((bf16[96,128]{1,0:T(8,128)(2,1)S(1)}, bf16[96,128]{1,0:T(8,128)(2,1)S(1)}, u32[]{:S(2)}, u32[]{:S(2)}) %collective-permute-start.7) | collective-permute-done | bytes 24608 | tf_op jit(solution)/shard_map/ppermute | solution.py:303
  73.8 0.0 copy-done.5
  73.8 0.0 copy-done.4
  73.8 1.6 %shard_map.108 = bf16[1,1,2,96,512]{4,3,2,1,0:T(8,128)(2,1)} custom-call(f32[96,1024]{1,0:T(8,128)S(1)} %get-tuple-element.37.partial, s32[1,1,2,2]{3,2,1,0:T(2,128)S(1)} %copy-done.4, s32[1,1,2,2]{3,2,1,0:T(2,128)S(1)} %copy-done.5, bf16[96,128]{1,0:T(8,128)(2,1)S(1)} %collective-permute-done.4.refs_0_.slab_far, ...), custom_call_target="tpu_custom_call" | custom-call | tf_op jit(solution)/shard_map/pallas_call | solution.py:398
  75.3 0.1 all-to-all-done.2
  75.4 1.0 %shard_map.109 = (f32[7,96,192]{2,1,0:T(8,128)}, f32[1,192]{1,0:T(1,128)}) custom-call(bf16[1024,128]{1,0:T(8,128)(2,1)S(1)} %bitcast.11), custom_call_target="tpu_custom_call" | custom-call | tf_op jit(solution)/shard_map/pallas_call | solution.py:413
Async XLA Ops:
  0.6 16.7 %copy-start.1 = (bf16[1,1,2,96,512]{4,3,2,1,0:T(8,128)(2,1)S(1)}, bf16[1,1,2,96,512]{4,3,2,1,0:T(8,128)(2,1)}, u32[]{:S(2)}) copy-start(bf16[1,1,2,96,512]{4,3,2,1,0:T(8,128)(2,1)} %features_in.3) | copy-start | bytes 589828
  2.6 14.0 %collective-permute-start = (bf16[96,128]{1,0:T(8,128)(2,1)}, bf16[96,128]{1,0:T(8,128)(2,1)S(1)}, u32[]{:S(2)}, u32[]{:S(2)}) collective-permute-start(bf16[96,128]{1,0:T(8,128)(2,1)} %get-tuple-element.23), channel_id=1, source_target_pairs={{4,8},{8,4},{12,16},{16,12},{20,24},{24,20},{28,32},{32,28},{36,40... | collective-permute-start | bytes 73736 | tf_op jit(solution)/shard_map/ppermute | solution.py:303
  3.3 13.4 %collective-permute-start.1 = (bf16[96,128]{1,0:T(8,128)(2,1)}, bf16[96,128]{1,0:T(8,128)(2,1)S(1)}, u32[]{:S(2)}, u32[]{:S(2)}) collective-permute-start(bf16[96,128]{1,0:T(8,128)(2,1)} %get-tuple-element.24), channel_id=1, source_target_pairs={{0,4},{4,0},{8,12},{12,8},{16,20},{20,16},{24,28},{28,24},{32,36},... | collective-permute-start | bytes 73736 | tf_op jit(solution)/shard_map/ppermute | solution.py:303
  9.7 7.0 %collective-permute-start.2 = (bf16[96,128]{1,0:T(8,128)(2,1)}, bf16[96,128]{1,0:T(8,128)(2,1)S(1)}, u32[]{:S(2)}, u32[]{:S(2)}) collective-permute-start(bf16[96,128]{1,0:T(8,128)(2,1)} %get-tuple-element.25), channel_id=1, source_target_pairs={{1,2},{2,1},{5,6},{6,5},{9,10},{10,9},{13,14},{14,13},{17,18},{18,... | collective-permute-start | bytes 73736 | tf_op jit(solution)/shard_map/ppermute | solution.py:303
  14.0 3.3 %collective-permute-start.3 = (bf16[96,128]{1,0:T(8,128)(2,1)}, bf16[96,128]{1,0:T(8,128)(2,1)S(1)}, u32[]{:S(2)}, u32[]{:S(2)}) collective-permute-start(bf16[96,128]{1,0:T(8,128)(2,1)} %get-tuple-element.26), channel_id=1, source_target_pairs={{0,1},{1,0},{2,3},{3,2},{4,5},{5,4},{6,7},{7,6},{8,9},{9,8},{10,11... | collective-permute-start | bytes 73736 | tf_op jit(solution)/shard_map/ppermute | solution.py:303
  15.9 1.4 %copy-start.6 = (f32[192]{0:T(256)S(1)}, f32[192]{0:T(256)}, u32[]{:S(2)}) copy-start(f32[192]{0:T(256)} %param.11) | copy-start | bytes 2308
  17.3 0.7 copy-start.3
  21.3 7.3 %copy-start = (bf16[7,96,192]{2,1,0:T(8,128)(2,1)S(1)}, bf16[7,96,192]{2,1,0:T(8,128)(2,1)}, u32[]{:S(2)}) copy-start(bf16[7,96,192]{2,1,0:T(8,128)(2,1)} %param.10) | copy-start | bytes 774148
  21.3 15.6 %all-to-all-start = ((bf16[32,32,128]{2,1,0:T(8,128)(2,1)}), bf16[32,32,128]{2,1,0:T(8,128)(2,1)S(1)}, u32[]{:S(2)}, u32[]{:S(2)}) async-start(bf16[32,32,128]{2,1,0:T(8,128)(2,1)} %bitcast.2), calls=%async_computation | async-start | bytes 524288 | tf_op jit(solution)/shard_map/all_to_all | solution.py:321
  28.6 1.0 %copy-start.2 = (bf16[256,1024]{1,0:T(8,128)(2,1)S(1)}, bf16[256,1024]{1,0:T(8,128)(2,1)}, u32[]{:S(2)}) copy-start(bf16[256,1024]{1,0:T(8,128)(2,1)} %get-tuple-element.28.grad) | copy-start | bytes 1572868
  37.6 24.0 %all-to-all-start.1 = ((bf16[16,32,128]{2,1,0:T(8,128)(2,1)}), bf16[16,32,128]{2,1,0:T(8,128)(2,1)S(1)}, u32[]{:S(2)}, u32[]{:S(2)}) async-start(bf16[16,32,128]{2,1,0:T(8,128)(2,1)} %bitcast.4), calls=%async_computation.1 | async-start | bytes 262144 | tf_op jit(solution)/shard_map/all_to_all | solution.py:321
  49.9 3.8 %collective-permute-start.4 = (bf16[96,128]{1,0:T(8,128)(2,1)S(1)}, bf16[96,128]{1,0:T(8,128)(2,1)S(1)}, u32[]{:S(2)}, u32[]{:S(2)}) collective-permute-start(bf16[96,128]{1,0:T(8,128)(2,1)S(1)} %get-tuple-element.32), channel_id=1, source_target_pairs={{4,8},{8,4},{12,16},{16,12},{20,24},{24,20},{28,32},{32,28},{36,40... | collective-permute-start | bytes 73736 | tf_op jit(solution)/shard_map/ppermute | solution.py:303
  50.6 4.9 %collective-permute-start.5 = (bf16[96,128]{1,0:T(8,128)(2,1)S(1)}, bf16[96,128]{1,0:T(8,128)(2,1)S(1)}, u32[]{:S(2)}, u32[]{:S(2)}) collective-permute-start(bf16[96,128]{1,0:T(8,128)(2,1)S(1)} %get-tuple-element.33), channel_id=1, source_target_pairs={{0,4},{4,0},{8,12},{12,8},{16,20},{20,16},{24,28},{28,24},{32,36},... | collective-permute-start | bytes 73736 | tf_op jit(solution)/shard_map/ppermute | solution.py:303
  62.3 13.1 %all-to-all-start.2 = ((bf16[32,32,128]{2,1,0:T(8,128)(2,1)}), bf16[32,32,128]{2,1,0:T(8,128)(2,1)S(1)}, u32[]{:S(2)}, u32[]{:S(2)}) async-start(bf16[32,32,128]{2,1,0:T(8,128)(2,1)} %bitcast.6), calls=%async_computation.2 | async-start | bytes 524288 | tf_op jit(solution)/shard_map/all_to_all | solution.py:321
  67.1 5.8 %collective-permute-start.6 = (bf16[96,128]{1,0:T(8,128)(2,1)S(1)}, bf16[96,128]{1,0:T(8,128)(2,1)S(1)}, u32[]{:S(2)}, u32[]{:S(2)}) collective-permute-start(bf16[96,128]{1,0:T(8,128)(2,1)S(1)} %get-tuple-element.38), channel_id=1, source_target_pairs={{1,2},{2,1},{5,6},{6,5},{9,10},{10,9},{13,14},{14,13},{17,18},{18,... | collective-permute-start | bytes 73736 | tf_op jit(solution)/shard_map/ppermute | solution.py:303
  70.7 3.1 %copy-start.5 = (s32[1,1,2,2]{3,2,1,0:T(2,128)S(1)}, s32[1,1,2,2]{3,2,1,0:T(2,128)}, u32[]{:S(2)}) copy-start(s32[1,1,2,2]{3,2,1,0:T(2,128)} %cross_in.3) | copy-start | bytes 52
  70.7 3.1 %copy-start.4 = (s32[1,1,2,2]{3,2,1,0:T(2,128)S(1)}, s32[1,1,2,2]{3,2,1,0:T(2,128)}, u32[]{:S(2)}) copy-start(s32[1,1,2,2]{3,2,1,0:T(2,128)} %slab_in.3) | copy-start | bytes 52
  70.7 3.1 %collective-permute-start.7 = (bf16[96,128]{1,0:T(8,128)(2,1)S(1)}, bf16[96,128]{1,0:T(8,128)(2,1)S(1)}, u32[]{:S(2)}, u32[]{:S(2)}) collective-permute-start(bf16[96,128]{1,0:T(8,128)(2,1)S(1)} %get-tuple-element.39), channel_id=1, source_target_pairs={{0,1},{1,0},{2,3},{3,2},{4,5},{5,4},{6,7},{7,6},{8,9},{9,8},{10,11... | collective-permute-start | bytes 73736 | tf_op jit(solution)/shard_map/ppermute | solution.py:303

commit v4 on v3

--- a/solution.py
+++ b/solution.py
@@ -190,9 +190,13 @@
                                        jnp.where(row == 1, found[depth:, TILE:], 0.0)).astype(bf16)
 
 
-def back_kernel(weights, grad, links_in, *refs):
-    sent, (partial, marks, table_grad, links, arrivals) = refs[:4], refs[4:]
-    copies = fetch((links_in,), (links,), arrivals)
+def list_places(number):
+    return [(axis, side, b, place) for axis in range(2) for side in range(2) for b in range(number) for place in range(2)]
+
+
+def back_kernel(weights, grad, links_in, slab_in, cross_in, *refs):
+    sent, (partial, flags, marks, table_grad, links, slab_list, cross_list, arrivals) = refs[:4], refs[4:]
+    copies = fetch((links_in, slab_in, cross_in), (links, slab_list, cross_list), arrivals)
     channels, total = partial.shape
     number = links.shape[2]
     voxels = total // number
@@ -205,7 +209,14 @@
     for axis in (1, 2):
         marks[TILE * (axis - 1):TILE * axis] = layer_map(axis, voxels)
     table_grad[...] = jnp.zeros(table_grad.shape, f32)
-    copies[0].wait()
+    for copy in copies:
+        copy.wait()
+    row = lax.broadcasted_iota(jnp.int32, flags.shape, 0)
+    named = jnp.zeros(flags.shape, f32)
+    for k, (axis, side, b, place) in enumerate(list_places(number)):
+        entry = (slab_list, cross_list)[axis][0, 0, 1 - side, place]
+        named = jnp.where((row == k) & (entry == 6 * b + 2 * axis + side), 1.0, named)
+    flags[...] = named
     live = grad[:out_channels]
     summed = nn(weights[:channels], live)
     for axis in range(3):
@@ -249,32 +260,26 @@
     shared[...] = jnp.broadcast_to(value[None], (parts, rows, TILE)).reshape(shared.shape)
 
 
-def finish_kernel(partial, slab_in, cross_in, slab_far, slab_near, cross_far, cross_near, result, marks, slab_list,
-                  cross_list, arrivals):
-    copies = fetch((slab_in, cross_in), (slab_list, cross_list), arrivals)
+def finish_kernel(scale, gathered, partial, flags, slab_far, slab_near, cross_far, cross_near,
+                  kernel_grad, bias_grad, result, marks):
+    unpack(scale, gathered, kernel_grad, bias_grad)
     number, channels, voxels = result.shape[2:]
     half = low_half(channels)
     marks[...] = layer_map(1, voxels)
-    for copy in copies:
-        copy.wait()
     second, first, cross_second, cross_first = from_peers((slab_far, slab_near, cross_far, cross_near))
-    groups = ((slab_list, (first, second)), (cross_list, (cross_first, cross_second)))
-    faces = [[doubled(back) for back in backs] for _, backs in groups]
+    faces = [[doubled(back) for back in backs] for backs in ((second, first), (cross_second, cross_first))]
+    sides = {}
+    for k, (axis, side, b, place) in enumerate(list_places(number)):
+        value = flags[k:k + 1] * faces[axis][side][place]
+        sides[axis, side, b] = sides[axis, side, b] + value if place else value
     for b in range(number):
         parts = partial[:, voxels * b:voxels * (b + 1)]
-        for axis, (listed, _) in enumerate(groups):
-            sides = []
-            for side in range(2):
-                value = jnp.zeros((channels, TILE), f32)
-                for k in range(2):
-                    entry = listed[0, 0, 1 - side, k]
-                    value = value + jnp.where(entry == 6 * b + 2 * axis + side, faces[axis][1 - side][k], 0.0)
-                sides.append(value)
-            parts = parts + spread(jnp.where(half, sides[0], sides[1]), axis, marks, voxels)
+        for axis in range(2):
+            parts = parts + spread(jnp.where(half, sides[axis, 0, b], sides[axis, 1, b]), axis, marks, voxels)
         result[0, 0, b] = parts.astype(bf16)
 
 
-def unpack_kernel(scale, gathered, kernel_grad, bias_grad):
+def unpack(scale, gathered, kernel_grad, bias_grad):
     taps, channels, out_channels = kernel_grad.shape
     depth = taps * channels
     middle = depth // 2
@@ -371,19 +376,21 @@
         compiler_params=middle,
     )(features, weights.reshape(depth, out_channels), out_grad, conv_bias.reshape(1, out_channels), brick_count,
       neighbours, *swap(*sends[:2], "slab"), *swap(*sends[2:], "cross"))
-    *backs, partial = pl.pallas_call(
+    *backs, partial, flags = pl.pallas_call(
         back_kernel,
-        out_shape=[face_pair] * 4 + [shape((channels, total), f32)],
-        in_specs=[VMEM, VMEM, HBM],
-        out_specs=[VMEM] * 5,
+        out_shape=[face_pair] * 4 + [shape((channels, total), f32), shape((len(list_places(number)), TILE), f32)],
+        in_specs=[VMEM, VMEM] + [HBM] * 3,
+        out_specs=[VMEM] * 6,
         scratch_shapes=[
             pltpu.VMEM((2 * TILE, voxels), bf16),
             pltpu.VMEM((6 * number + 9, channels, TILE), f32),
             pltpu.SMEM(neighbours.shape, jnp.int32),
-            pltpu.SemaphoreType.DMA((1,)),
+            pltpu.SMEM(send_slab.shape, jnp.int32),
+            pltpu.SMEM(send_cross.shape, jnp.int32),
+            pltpu.SemaphoreType.DMA((3,)),
         ],
         compiler_params=small,
-    )(weights.reshape(depth, out_channels), grad, neighbours)
+    )(weights.reshape(depth, out_channels), grad, neighbours, send_slab, send_cross)
 
     near = NEAR if owners == 512 else tuple(range(owners.bit_length() // 2))
     far = tuple(bit for bit in range(owners.bit_length() - 1) if bit not in near)
@@ -395,28 +402,16 @@
     shared, passed = staged_sum(
         arrived, packed.shape[0], 1 << len(near), slab_back, [partial, *backs[2:]], small)
     partial, cross_back = passed[0], swap(*passed[1:], "cross")
-    grad_features = pl.pallas_call(
-        finish_kernel,
-        out_shape=shape(features.shape, bf16),
-        in_specs=[VMEM, HBM, HBM] + [VMEM] * 4,
-        out_specs=VMEM,
-        scratch_shapes=[
-            pltpu.VMEM((TILE, voxels), bf16),
-            pltpu.SMEM(send_slab.shape, jnp.int32),
-            pltpu.SMEM(send_cross.shape, jnp.int32),
-            pltpu.SemaphoreType.DMA((2,)),
-        ],
-        compiler_params=small,
-    )(partial, send_slab, send_cross, *slab_back, *cross_back)
     gathered = exchange(shared, near, owners)
     scale = 1.0 / math.sqrt(owners * total)
-    kernel_grad, bias_grad = pl.pallas_call(
-        lambda *refs: unpack_kernel(scale, *refs),
-        out_shape=[shape(weights.shape, f32), shape((1, out_channels), f32)],
-        in_specs=[VMEM],
-        out_specs=[VMEM] * 2,
+    kernel_grad, bias_grad, grad_features = pl.pallas_call(
+        lambda *refs: finish_kernel(scale, *refs),
+        out_shape=[shape(weights.shape, f32), shape((1, out_channels), f32), shape(features.shape, bf16)],
+        in_specs=[VMEM] * 7,
+        out_specs=[VMEM] * 3,
+        scratch_shapes=[pltpu.VMEM((TILE, voxels), bf16)],
         compiler_params=small,
-    )(gathered)
+    )(gathered, partial, flags, *slab_back, *cross_back)
     return grad_features, kernel_grad, bias_grad.reshape(out_channels)
 
 

time: 77.1 us -> 77.4 us (level)
  Pallas kernels: 11.1 us -> 9.9 us
  waiting for transfers between devices: 15.1 us -> 16 us
    pallas_call x2 -> x1, Pallas kernels: 2.52 us -> 1.26 us  [local(): pl.pallas_call(lambda *refs: finish_kernel(scale, *refs), out_shape=[shap...]
    all_to_all x3, waiting for transfers between devices: 11.6 us -> 12.4 us  [exchange(): lax.all_to_all(value, ('slab', 'cross'), 0, 0, axis_index_groups=groups_o...]
  transfers between devices with their start and end apart: 11 -> 11, of which waited for: 7 -> 7; matrix products, arithmetic and copies ran while one was open for 0% -> 0% of each run, Pallas kernels for 5% -> 3%
where the time goes in v4:
time: 77.4 us; the launch traced here: 76.7 us
  starting transfers between devices  47 us (61%)
  waiting for transfers between devices  16 us (21%)
  Pallas kernels  9.9 us (13%)
  local copies, waits for them, and re-layouts  2.39 us (3%)
  between operations  1.49 us (2%)
    all_to_all x3, starting transfers between devices, exchange(): lax.all_to_all(value, ('slab', 'cross'), 0, 0, axis_index_groups=groups_o...  24.4 us
    ppermute x8, starting transfers between devices, pairs(): lax.ppermute(value, axis, [pair for low in lows for pair in ((low, low +...  22.6 us
    all_to_all x3, waiting for transfers between devices, exchange(): lax.all_to_all(value, ('slab', 'cross'), 0, 0, axis_index_groups=groups_o...  12.4 us
    ppermute x8, waiting for transfers between devices, pairs(): lax.ppermute(value, axis, [pair for low in lows for pair in ((low, low +...  3.54 us
    pallas_call x1, Pallas kernels, local(): pl.pallas_call(main_kernel, out_shape=[packed, shape((2 * TILE, total), b...  3.27 us
    unnamed x14, local copies, waits for them, and re-layouts  2.39 us
    pallas_call x1, Pallas kernels, local(): pl.pallas_call(back_kernel, out_shape=[face_pair] * 4 + [shape((channels,...  1.97 us
    pallas_call x1, Pallas kernels, local(): pl.pallas_call(send_kernel, out_shape=[face_pair] * 4, in_specs=[HBM] * 3...  1.96 us
  transfers between devices with their start and end apart: 11, of which 7 were waited for; matrix products, arithmetic and copies ran while one was open for 0% of the time, Pallas kernels for 3%

profile of v4, /device:TPU:1, one launch (start us, length us, event | category | flops | bytes accessed | tf_op | source)
XLA Modules:
  0.0 76.7 jit_solution(12858705601864169902)
XLA Ops:
  0.6 0.0 copy-start.1
  0.6 2.0 %shard_map.103 = (bf16[96,128]{1,0:T(8,128)(2,1)}, bf16[96,128]{1,0:T(8,128)(2,1)}, bf16[96,128]{1,0:T(8,128)(2,1)}, bf16[96,128]{1,0:T(8,128)(2,1)}) custom-call(bf16[1,1,2,96,512]{4,3,2,1,0:T(8,128)(2,1)} %features_in.3, s32[1,1,2,2]{3,2,1,0:T(2,128)} %slab_in.3, s32[1,1,2,2]{3,2,1,0:T(2,128)} %cross_in.3), custom_call_target="tpu_custom_call" | custom-call | tf_op jit(solution)/shard_map/pallas_call | solution.py:344
  2.6 0.7 collective-permute-start
  3.3 6.4 %collective-permute-start.1 = (bf16[96,128]{1,0:T(8,128)(2,1)}, bf16[96,128]{1,0:T(8,128)(2,1)S(1)}, u32[]{:S(2)}, u32[]{:S(2)}) collective-permute-start(bf16[96,128]{1,0:T(8,128)(2,1)} %get-tuple-element.26), channel_id=1, source_target_pairs={{0,4},{4,0},{8,12},{12,8},{16,20},{20,16},{24,28},{28,24},{32,36},... | collective-permute-start | bytes 73736 | tf_op jit(solution)/shard_map/ppermute | solution.py:308
  9.7 4.3 %collective-permute-start.2 = (bf16[96,128]{1,0:T(8,128)(2,1)}, bf16[96,128]{1,0:T(8,128)(2,1)S(1)}, u32[]{:S(2)}, u32[]{:S(2)}) collective-permute-start(bf16[96,128]{1,0:T(8,128)(2,1)} %get-tuple-element.27), channel_id=1, source_target_pairs={{1,2},{2,1},{5,6},{6,5},{9,10},{10,9},{13,14},{14,13},{17,18},{18,... | collective-permute-start | bytes 73736 | tf_op jit(solution)/shard_map/ppermute | solution.py:308
  14.0 1.9 %collective-permute-start.3 = (bf16[96,128]{1,0:T(8,128)(2,1)}, bf16[96,128]{1,0:T(8,128)(2,1)S(1)}, u32[]{:S(2)}, u32[]{:S(2)}) collective-permute-start(bf16[96,128]{1,0:T(8,128)(2,1)} %get-tuple-element.28), channel_id=1, source_target_pairs={{0,1},{1,0},{2,3},{3,2},{4,5},{5,4},{6,7},{7,6},{8,9},{9,8},{10,11... | collective-permute-start | bytes 73736 | tf_op jit(solution)/shard_map/ppermute | solution.py:308
  15.9 0.0 copy-start.6
  16.6 0.0 collective-permute-done.refs_0_
  16.6 0.0 collective-permute-done.1.refs_1_
  16.6 0.0 collective-permute-done.2.refs_2_
  16.6 0.7 collective-permute-done.3.refs_3_
  17.3 0.0 copy-start.3
  17.3 0.0 copy-done.1
  17.3 0.0 copy-done.6
  17.3 0.7 copy-done.3
  18.0 3.3 %shard_map.104 = (bf16[1024,128]{1,0:T(8,128)(2,1)}, bf16[256,1024]{1,0:T(8,128)(2,1)}) custom-call(bf16[1,1,2,96,512]{4,3,2,1,0:T(8,128)(2,1)S(1)} %copy-done.1, bf16[672,192]{1,0:T(8,128)(2,1)} %bitcast.9, bf16[1,1,2,192,512]{4,3,2,1,0:T(8,128)(2,1)} %upstream_in.1, f32[1,192]{1,0:T(1,128)S(1)} %bitcast.14, s32[1,1]{1,0:T(1,128)S(6)} %copy.21.count_in, ...), custom_call_target="tpu_custom_call" | custom-call | tf_op jit(solution)/shard_map/pallas_call | solution.py:358
  21.3 0.0 copy-start
  21.3 0.0 copy-start.5
  21.3 7.3 %all-to-all-start = ((bf16[32,32,128]{2,1,0:T(8,128)(2,1)}), bf16[32,32,128]{2,1,0:T(8,128)(2,1)S(1)}, u32[]{:S(2)}, u32[]{:S(2)}) async-start(bf16[32,32,128]{2,1,0:T(8,128)(2,1)} %bitcast.2), calls=%async_computation | async-start | bytes 524288 | tf_op jit(solution)/shard_map/all_to_all | solution.py:326
  28.6 0.0 copy-start.4
  28.6 0.0 copy-done
  28.6 0.0 copy-done.5
  28.6 0.7 copy-done.4
  29.3 0.0 copy-start.2
  29.3 1.0 %copy-done.2 = bf16[256,1024]{1,0:T(8,128)(2,1)S(1)} copy-done((bf16[256,1024]{1,0:T(8,128)(2,1)S(1)}, bf16[256,1024]{1,0:T(8,128)(2,1)}, u32[]{:S(2)}) %copy-start.2) | copy-done | bytes 524312
  30.3 2.0 %shard_map.105 = (bf16[96,128]{1,0:T(8,128)(2,1)S(1)}, bf16[96,128]{1,0:T(8,128)(2,1)S(1)}, bf16[96,128]{1,0:T(8,128)(2,1)S(1)}, bf16[96,128]{1,0:T(8,128)(2,1)S...) custom-call(bf16[672,192]{1,0:T(8,128)(2,1)S(1)} %bitcast.10, bf16[256,1024]{1,0:T(8,128)(2,1)S(1)} %copy-done.2, ...), custom_call_target="tpu_custom_call" | custom-call | tf_op jit(solution)/shard_map/pallas_call | solution.py:379
  32.3 4.6 %all-to-all-done = bf16[32,32,128]{2,1,0:T(8,128)(2,1)S(1)} async-done(((bf16[32,32,128]{2,1,0:T(8,128)(2,1)}), bf16[32,32,128]{2,1,0:T(8,128)(2,1)S(1)}, u32[]{:S(2)}, u32[]{:S(2)}) %all-to-all-start) | async-done | bytes 262176 | tf_op jit(solution)/shard_map/all_to_all | solution.py:326
  36.9 0.7 shard_map.106
  37.6 12.3 %all-to-all-start.1 = ((bf16[16,32,128]{2,1,0:T(8,128)(2,1)}), bf16[16,32,128]{2,1,0:T(8,128)(2,1)S(1)}, u32[]{:S(2)}, u32[]{:S(2)}) async-start(bf16[16,32,128]{2,1,0:T(8,128)(2,1)} %bitcast.4), calls=%async_computation.1 | async-start | bytes 262144 | tf_op jit(solution)/shard_map/all_to_all | solution.py:326
  50.0 0.7 collective-permute-start.4
  50.6 3.1 %collective-permute-start.5 = (bf16[96,128]{1,0:T(8,128)(2,1)S(1)}, bf16[96,128]{1,0:T(8,128)(2,1)S(1)}, u32[]{:S(2)}, u32[]{:S(2)}) collective-permute-start(bf16[96,128]{1,0:T(8,128)(2,1)S(1)} %get-tuple-element.35), channel_id=1, source_target_pairs={{0,4},{4,0},{8,12},{12,8},{16,20},{20,16},{24,28},{28,24},{32,36},... | collective-permute-start | bytes 73736 | tf_op jit(solution)/shard_map/ppermute | solution.py:308
  53.8 0.0 collective-permute-done.4.refs_0_.refs_3_
  53.8 1.7 %collective-permute-done.5.refs_1_.refs_4_ = bf16[96,128]{1,0:T(8,128)(2,1)S(1)} collective-permute-done((bf16[96,128]{1,0:T(8,128)(2,1)S(1)}, bf16[96,128]{1,0:T(8,128)(2,1)S(1)}, u32[]{:S(2)}, u32[]{:S(2)}) %collective-permute-start.5) | collective-permute-done | bytes 24608 | tf_op jit(solution)/shard_map/ppermute | solution.py:308
  55.5 6.1 %all-to-all-done.1 = bf16[16,32,128]{2,1,0:T(8,128)(2,1)S(1)} async-done(((bf16[16,32,128]{2,1,0:T(8,128)(2,1)}), bf16[16,32,128]{2,1,0:T(8,128)(2,1)S(1)}, u32[]{:S(2)}, u32[]{:S(2)}) %all-to-all-start.1) | async-done | bytes 131104 | tf_op jit(solution)/shard_map/all_to_all | solution.py:326
  61.6 0.7 shard_map.107
  62.3 4.8 %all-to-all-start.2 = ((bf16[32,32,128]{2,1,0:T(8,128)(2,1)}), bf16[32,32,128]{2,1,0:T(8,128)(2,1)S(1)}, u32[]{:S(2)}, u32[]{:S(2)}) async-start(bf16[32,32,128]{2,1,0:T(8,128)(2,1)} %bitcast.6), calls=%async_computation.2 | async-start | bytes 524288 | tf_op jit(solution)/shard_map/all_to_all | solution.py:326
  67.1 3.5 %collective-permute-start.6 = (bf16[96,128]{1,0:T(8,128)(2,1)S(1)}, bf16[96,128]{1,0:T(8,128)(2,1)S(1)}, u32[]{:S(2)}, u32[]{:S(2)}) collective-permute-start(bf16[96,128]{1,0:T(8,128)(2,1)S(1)} %get-tuple-element.42), channel_id=1, source_target_pairs={{1,2},{2,1},{5,6},{6,5},{9,10},{10,9},{13,14},{14,13},{17,18},{18,... | collective-permute-start | bytes 73736 | tf_op jit(solution)/shard_map/ppermute | solution.py:308
  70.7 1.9 %collective-permute-start.7 = (bf16[96,128]{1,0:T(8,128)(2,1)S(1)}, bf16[96,128]{1,0:T(8,128)(2,1)S(1)}, u32[]{:S(2)}, u32[]{:S(2)}) collective-permute-start(bf16[96,128]{1,0:T(8,128)(2,1)S(1)} %get-tuple-element.43), channel_id=1, source_target_pairs={{0,1},{1,0},{2,3},{3,2},{4,5},{5,4},{6,7},{7,6},{8,9},{9,8},{10,11... | collective-permute-start | bytes 73736 | tf_op jit(solution)/shard_map/ppermute | solution.py:308
  72.6 0.3 collective-permute-done.6.refs_5_
  72.9 0.8 %collective-permute-done.7.refs_6_ = bf16[96,128]{1,0:T(8,128)(2,1)S(1)} collective-permute-done((bf16[96,128]{1,0:T(8,128)(2,1)S(1)}, bf16[96,128]{1,0:T(8,128)(2,1)S(1)}, u32[]{:S(2)}, u32[]{:S(2)}) %collective-permute-start.7) | collective-permute-done | bytes 24608 | tf_op jit(solution)/shard_map/ppermute | solution.py:308
  73.8 1.7 %all-to-all-done.2 = bf16[32,32,128]{2,1,0:T(8,128)(2,1)S(1)} async-done(((bf16[32,32,128]{2,1,0:T(8,128)(2,1)}), bf16[32,32,128]{2,1,0:T(8,128)(2,1)S(1)}, u32[]{:S(2)}, u32[]{:S(2)}) %all-to-all-start.2) | async-done | bytes 262176 | tf_op jit(solution)/shard_map/all_to_all | solution.py:326
  75.5 1.3 %shard_map.108 = (f32[7,96,192]{2,1,0:T(8,128)}, f32[1,192]{1,0:T(1,128)}, bf16[1,1,2,96,512]{4,3,2,1,0:T(8,128)(2,1)}) custom-call(bf16[1024,128]{1,0:T(8,128)(2,1)S(1)} %bitcast.11, f32[96,1024]{1,0:T(8,128)S(1)} %get-tuple-element.40.refs_1_, f32[16,128]{1,0:T(8,128)S(1)} %get-tuple-element.41.refs_2_, ...), custom_call_target="tpu_custom_call" | custom-call | tf_op jit(solution)/shard_map/pallas_call | solution.py:407
Async XLA Ops:
  0.6 16.7 %copy-start.1 = (bf16[1,1,2,96,512]{4,3,2,1,0:T(8,128)(2,1)S(1)}, bf16[1,1,2,96,512]{4,3,2,1,0:T(8,128)(2,1)}, u32[]{:S(2)}) copy-start(bf16[1,1,2,96,512]{4,3,2,1,0:T(8,128)(2,1)} %features_in.3) | copy-start | bytes 589828
  2.6 14.0 %collective-permute-start = (bf16[96,128]{1,0:T(8,128)(2,1)}, bf16[96,128]{1,0:T(8,128)(2,1)S(1)}, u32[]{:S(2)}, u32[]{:S(2)}) collective-permute-start(bf16[96,128]{1,0:T(8,128)(2,1)} %get-tuple-element.25), channel_id=1, source_target_pairs={{4,8},{8,4},{12,16},{16,12},{20,24},{24,20},{28,32},{32,28},{36,40... | collective-permute-start | bytes 73736 | tf_op jit(solution)/shard_map/ppermute | solution.py:308
  3.3 13.4 %collective-permute-start.1 = (bf16[96,128]{1,0:T(8,128)(2,1)}, bf16[96,128]{1,0:T(8,128)(2,1)S(1)}, u32[]{:S(2)}, u32[]{:S(2)}) collective-permute-start(bf16[96,128]{1,0:T(8,128)(2,1)} %get-tuple-element.26), channel_id=1, source_target_pairs={{0,4},{4,0},{8,12},{12,8},{16,20},{20,16},{24,28},{28,24},{32,36},... | collective-permute-start | bytes 73736 | tf_op jit(solution)/shard_map/ppermute | solution.py:308
  9.7 7.0 %collective-permute-start.2 = (bf16[96,128]{1,0:T(8,128)(2,1)}, bf16[96,128]{1,0:T(8,128)(2,1)S(1)}, u32[]{:S(2)}, u32[]{:S(2)}) collective-permute-start(bf16[96,128]{1,0:T(8,128)(2,1)} %get-tuple-element.27), channel_id=1, source_target_pairs={{1,2},{2,1},{5,6},{6,5},{9,10},{10,9},{13,14},{14,13},{17,18},{18,... | collective-permute-start | bytes 73736 | tf_op jit(solution)/shard_map/ppermute | solution.py:308
  14.0 3.3 %collective-permute-start.3 = (bf16[96,128]{1,0:T(8,128)(2,1)}, bf16[96,128]{1,0:T(8,128)(2,1)S(1)}, u32[]{:S(2)}, u32[]{:S(2)}) collective-permute-start(bf16[96,128]{1,0:T(8,128)(2,1)} %get-tuple-element.28), channel_id=1, source_target_pairs={{0,1},{1,0},{2,3},{3,2},{4,5},{5,4},{6,7},{7,6},{8,9},{9,8},{10,11... | collective-permute-start | bytes 73736 | tf_op jit(solution)/shard_map/ppermute | solution.py:308
  15.9 1.4 %copy-start.6 = (f32[192]{0:T(256)S(1)}, f32[192]{0:T(256)}, u32[]{:S(2)}) copy-start(f32[192]{0:T(256)} %param.11) | copy-start | bytes 2308
  17.3 0.7 copy-start.3
  21.3 7.3 %copy-start = (bf16[7,96,192]{2,1,0:T(8,128)(2,1)S(1)}, bf16[7,96,192]{2,1,0:T(8,128)(2,1)}, u32[]{:S(2)}) copy-start(bf16[7,96,192]{2,1,0:T(8,128)(2,1)} %param.10) | copy-start | bytes 774148
  21.3 7.3 %copy-start.5 = (s32[1,1,2,2]{3,2,1,0:T(2,128)S(1)}, s32[1,1,2,2]{3,2,1,0:T(2,128)}, u32[]{:S(2)}) copy-start(s32[1,1,2,2]{3,2,1,0:T(2,128)} %cross_in.3) | copy-start | bytes 52
  21.3 15.6 %all-to-all-start = ((bf16[32,32,128]{2,1,0:T(8,128)(2,1)}), bf16[32,32,128]{2,1,0:T(8,128)(2,1)S(1)}, u32[]{:S(2)}, u32[]{:S(2)}) async-start(bf16[32,32,128]{2,1,0:T(8,128)(2,1)} %bitcast.2), calls=%async_computation | async-start | bytes 524288 | tf_op jit(solution)/shard_map/all_to_all | solution.py:326
  28.6 0.7 copy-start.4
  29.3 1.0 %copy-start.2 = (bf16[256,1024]{1,0:T(8,128)(2,1)S(1)}, bf16[256,1024]{1,0:T(8,128)(2,1)}, u32[]{:S(2)}) copy-start(bf16[256,1024]{1,0:T(8,128)(2,1)} %get-tuple-element.30.grad) | copy-start | bytes 1572868
  37.6 24.0 %all-to-all-start.1 = ((bf16[16,32,128]{2,1,0:T(8,128)(2,1)}), bf16[16,32,128]{2,1,0:T(8,128)(2,1)S(1)}, u32[]{:S(2)}, u32[]{:S(2)}) async-start(bf16[16,32,128]{2,1,0:T(8,128)(2,1)} %bitcast.4), calls=%async_computation.1 | async-start | bytes 262144 | tf_op jit(solution)/shard_map/all_to_all | solution.py:326
  50.0 3.8 %collective-permute-start.4 = (bf16[96,128]{1,0:T(8,128)(2,1)S(1)}, bf16[96,128]{1,0:T(8,128)(2,1)S(1)}, u32[]{:S(2)}, u32[]{:S(2)}) collective-permute-start(bf16[96,128]{1,0:T(8,128)(2,1)S(1)} %get-tuple-element.34), channel_id=1, source_target_pairs={{4,8},{8,4},{12,16},{16,12},{20,24},{24,20},{28,32},{32,28},{36,40... | collective-permute-start | bytes 73736 | tf_op jit(solution)/shard_map/ppermute | solution.py:308
  50.6 4.9 %collective-permute-start.5 = (bf16[96,128]{1,0:T(8,128)(2,1)S(1)}, bf16[96,128]{1,0:T(8,128)(2,1)S(1)}, u32[]{:S(2)}, u32[]{:S(2)}) collective-permute-start(bf16[96,128]{1,0:T(8,128)(2,1)S(1)} %get-tuple-element.35), channel_id=1, source_target_pairs={{0,4},{4,0},{8,12},{12,8},{16,20},{20,16},{24,28},{28,24},{32,36},... | collective-permute-start | bytes 73736 | tf_op jit(solution)/shard_map/ppermute | solution.py:308
  62.3 13.1 %all-to-all-start.2 = ((bf16[32,32,128]{2,1,0:T(8,128)(2,1)}), bf16[32,32,128]{2,1,0:T(8,128)(2,1)S(1)}, u32[]{:S(2)}, u32[]{:S(2)}) async-start(bf16[32,32,128]{2,1,0:T(8,128)(2,1)} %bitcast.6), calls=%async_computation.2 | async-start | bytes 524288 | tf_op jit(solution)/shard_map/all_to_all | solution.py:326
  67.1 5.8 %collective-permute-start.6 = (bf16[96,128]{1,0:T(8,128)(2,1)S(1)}, bf16[96,128]{1,0:T(8,128)(2,1)S(1)}, u32[]{:S(2)}, u32[]{:S(2)}) collective-permute-start(bf16[96,128]{1,0:T(8,128)(2,1)S(1)} %get-tuple-element.42), channel_id=1, source_target_pairs={{1,2},{2,1},{5,6},{6,5},{9,10},{10,9},{13,14},{14,13},{17,18},{18,... | collective-permute-start | bytes 73736 | tf_op jit(solution)/shard_map/ppermute | solution.py:308
  70.7 3.1 %collective-permute-start.7 = (bf16[96,128]{1,0:T(8,128)(2,1)S(1)}, bf16[96,128]{1,0:T(8,128)(2,1)S(1)}, u32[]{:S(2)}, u32[]{:S(2)}) collective-permute-start(bf16[96,128]{1,0:T(8,128)(2,1)S(1)} %get-tuple-element.43), channel_id=1, source_target_pairs={{0,1},{1,0},{2,3},{3,2},{4,5},{5,4},{6,7},{7,6},{8,9},{9,8},{10,11... | collective-permute-start | bytes 73736 | tf_op jit(solution)/shard_map/ppermute | solution.py:308

commit v5 on v4

--- a/solution.py
+++ b/solution.py
@@ -310,6 +310,11 @@
     return pairs(far, 1), pairs(near, 0)
 
 
+def swap_one(value, axis, first):
+    lows = range(first, lax.axis_size(axis) - 1, 2)
+    return lax.ppermute(value, axis, [pair for low in lows for pair in ((low, low + 1), (low + 1, low))])
+
+
 def staged_sum(arrived, rows, parts, ended, passed, params):
     shared, *passed = pl.pallas_call(
         lambda arrived, *refs: sum_chunks(arrived, refs[len(ended) + len(passed)], parts),
@@ -395,13 +400,14 @@
     near = NEAR if owners == 512 else tuple(range(owners.bit_length() // 2))
     far = tuple(bit for bit in range(owners.bit_length() - 1) if bit not in near)
     arrived = exchange(terms, near, owners)
-    shared, slab_back = staged_sum(
-        arrived, packed.shape[0] >> len(near) << len(far), 1 << len(far), [], backs[:2], small)
+    shared, (slab_far, cross_far) = staged_sum(
+        arrived, packed.shape[0] >> len(near) << len(far), 1 << len(far), [], [backs[0], backs[2]], small)
     arrived = exchange(shared, far, owners)
-    slab_back = swap(*slab_back, "slab")
-    shared, passed = staged_sum(
-        arrived, packed.shape[0], 1 << len(near), slab_back, [partial, *backs[2:]], small)
-    partial, cross_back = passed[0], swap(*passed[1:], "cross")
+    back_far = [swap_one(slab_far, "slab", 1), swap_one(cross_far, "cross", 1)]
+    shared, (partial, slab_near, cross_near) = staged_sum(
+        arrived, packed.shape[0], 1 << len(near), back_far, [partial, backs[1], backs[3]], small)
+    slab_back = back_far[0], swap_one(slab_near, "slab", 0)
+    cross_back = back_far[1], swap_one(cross_near, "cross", 0)
     gathered = exchange(shared, near, owners)
     scale = 1.0 / math.sqrt(owners * total)
     kernel_grad, bias_grad, grad_features = pl.pallas_call(

time: 77.4 us -> 77.4 us (level)
    ppermute x0 -> x4, starting transfers between devices: none -> 9.65 us  [swap_one(): lax.ppermute(value, axis, [pair for low in lows for pair in ((low, low +...]
    ppermute x8 -> x4, starting transfers between devices: 22.6 us -> 13.3 us  [pairs(): lax.ppermute(value, axis, [pair for low in lows for pair in ((low, low +...]
    ppermute x0 -> x4, waiting for transfers between devices: none -> 3.2 us  [swap_one(): lax.ppermute(value, axis, [pair for low in lows for pair in ((low, low +...]
    ppermute x8 -> x4, waiting for transfers between devices: 3.54 us -> 0.68 us  [pairs(): lax.ppermute(value, axis, [pair for low in lows for pair in ((low, low +...]
where the time goes in v5:
time: 77.4 us; the launch traced here: 76.7 us
  starting transfers between devices  47.3 us (61%)
  waiting for transfers between devices  15.6 us (20%)
  Pallas kernels  9.9 us (13%)
  local copies, waits for them, and re-layouts  2.39 us (3%)
  between operations  1.49 us (2%)
    all_to_all x3, starting transfers between devices, exchange(): lax.all_to_all(value, ('slab', 'cross'), 0, 0, axis_index_groups=groups_o...  24.4 us
    ppermute x4, starting transfers between devices, pairs(): lax.ppermute(value, axis, [pair for low in lows for pair in ((low, low +...  13.3 us
    all_to_all x3, waiting for transfers between devices, exchange(): lax.all_to_all(value, ('slab', 'cross'), 0, 0, axis_index_groups=groups_o...  11.7 us
    ppermute x4, starting transfers between devices, swap_one(): lax.ppermute(value, axis, [pair for low in lows for pair in ((low, low +...  9.65 us
    pallas_call x1, Pallas kernels, local(): pl.pallas_call(main_kernel, out_shape=[packed, shape((2 * TILE, total), b...  3.27 us
    ppermute x4, waiting for transfers between devices, swap_one(): lax.ppermute(value, axis, [pair for low in lows for pair in ((low, low +...  3.2 us
    unnamed x14, local copies, waits for them, and re-layouts  2.39 us
    pallas_call x1, Pallas kernels, local(): pl.pallas_call(back_kernel, out_shape=[face_pair] * 4 + [shape((channels,...  1.97 us
  transfers between devices with their start and end apart: 11, of which 7 were waited for; matrix products, arithmetic and copies ran while one was open for 0% of the time, Pallas kernels for 3%

profile of v5, /device:TPU:1, one launch (start us, length us, event | category | flops | bytes accessed | tf_op | source)
XLA Modules:
  0.0 76.7 jit_solution(15859420970950116769)
XLA Ops:
  0.6 0.0 copy-start.1
  0.6 2.0 %shard_map.103 = (bf16[96,128]{1,0:T(8,128)(2,1)}, bf16[96,128]{1,0:T(8,128)(2,1)}, bf16[96,128]{1,0:T(8,128)(2,1)}, bf16[96,128]{1,0:T(8,128)(2,1)}) custom-call(bf16[1,1,2,96,512]{4,3,2,1,0:T(8,128)(2,1)} %features_in.3, s32[1,1,2,2]{3,2,1,0:T(2,128)} %slab_in.3, s32[1,1,2,2]{3,2,1,0:T(2,128)} %cross_in.3), custom_call_target="tpu_custom_call" | custom-call | tf_op jit(solution)/shard_map/pallas_call | solution.py:349
  2.6 0.7 collective-permute-start
  3.3 6.4 %collective-permute-start.1 = (bf16[96,128]{1,0:T(8,128)(2,1)}, bf16[96,128]{1,0:T(8,128)(2,1)S(1)}, u32[]{:S(2)}, u32[]{:S(2)}) collective-permute-start(bf16[96,128]{1,0:T(8,128)(2,1)} %get-tuple-element.26), channel_id=1, source_target_pairs={{0,4},{4,0},{8,12},{12,8},{16,20},{20,16},{24,28},{28,24},{32,36},... | collective-permute-start | bytes 73736 | tf_op jit(solution)/shard_map/ppermute | solution.py:308
  9.7 4.3 %collective-permute-start.2 = (bf16[96,128]{1,0:T(8,128)(2,1)}, bf16[96,128]{1,0:T(8,128)(2,1)S(1)}, u32[]{:S(2)}, u32[]{:S(2)}) collective-permute-start(bf16[96,128]{1,0:T(8,128)(2,1)} %get-tuple-element.27), channel_id=1, source_target_pairs={{1,2},{2,1},{5,6},{6,5},{9,10},{10,9},{13,14},{14,13},{17,18},{18,... | collective-permute-start | bytes 73736 | tf_op jit(solution)/shard_map/ppermute | solution.py:308
  14.0 1.9 %collective-permute-start.3 = (bf16[96,128]{1,0:T(8,128)(2,1)}, bf16[96,128]{1,0:T(8,128)(2,1)S(1)}, u32[]{:S(2)}, u32[]{:S(2)}) collective-permute-start(bf16[96,128]{1,0:T(8,128)(2,1)} %get-tuple-element.28), channel_id=1, source_target_pairs={{0,1},{1,0},{2,3},{3,2},{4,5},{5,4},{6,7},{7,6},{8,9},{9,8},{10,11... | collective-permute-start | bytes 73736 | tf_op jit(solution)/shard_map/ppermute | solution.py:308
  15.9 0.0 copy-start.6
  16.6 0.0 collective-permute-done.refs_0_
  16.6 0.0 collective-permute-done.1.refs_1_
  16.6 0.0 collective-permute-done.2.refs_2_
  16.6 0.7 collective-permute-done.3.refs_3_
  17.3 0.0 copy-start.3
  17.3 0.0 copy-done.1
  17.3 0.0 copy-done.6
  17.3 0.7 copy-done.3
  18.0 3.3 %shard_map.104 = (bf16[1024,128]{1,0:T(8,128)(2,1)}, bf16[256,1024]{1,0:T(8,128)(2,1)}) custom-call(bf16[1,1,2,96,512]{4,3,2,1,0:T(8,128)(2,1)S(1)} %copy-done.1, bf16[672,192]{1,0:T(8,128)(2,1)} %bitcast.9, bf16[1,1,2,192,512]{4,3,2,1,0:T(8,128)(2,1)} %upstream_in.1, f32[1,192]{1,0:T(1,128)S(1)} %bitcast.14, s32[1,1]{1,0:T(1,128)S(6)} %copy.21.count_in, ...), custom_call_target="tpu_custom_call" | custom-call | tf_op jit(solution)/shard_map/pallas_call | solution.py:363
  21.3 0.0 copy-start
  21.3 0.0 copy-start.5
  21.3 7.3 %all-to-all-start = ((bf16[32,32,128]{2,1,0:T(8,128)(2,1)}), bf16[32,32,128]{2,1,0:T(8,128)(2,1)S(1)}, u32[]{:S(2)}, u32[]{:S(2)}) async-start(bf16[32,32,128]{2,1,0:T(8,128)(2,1)} %bitcast.2), calls=%async_computation | async-start | bytes 524288 | tf_op jit(solution)/shard_map/all_to_all | solution.py:331
  28.6 0.0 copy-start.4
  28.6 0.0 copy-done
  28.6 0.0 copy-done.5
  28.6 0.7 copy-done.4
  29.3 0.0 copy-start.2
  29.3 1.0 %copy-done.2 = bf16[256,1024]{1,0:T(8,128)(2,1)S(1)} copy-done((bf16[256,1024]{1,0:T(8,128)(2,1)S(1)}, bf16[256,1024]{1,0:T(8,128)(2,1)}, u32[]{:S(2)}) %copy-start.2) | copy-done | bytes 524312
  30.3 2.0 %shard_map.105 = (bf16[96,128]{1,0:T(8,128)(2,1)S(1)}, bf16[96,128]{1,0:T(8,128)(2,1)S(1)}, bf16[96,128]{1,0:T(8,128)(2,1)S(1)}, bf16[96,128]{1,0:T(8,128)(2,1)S...) custom-call(bf16[672,192]{1,0:T(8,128)(2,1)S(1)} %bitcast.10, bf16[256,1024]{1,0:T(8,128)(2,1)S(1)} %copy-done.2, ...), custom_call_target="tpu_custom_call" | custom-call | tf_op jit(solution)/shard_map/pallas_call | solution.py:384
  32.3 4.6 %all-to-all-done = bf16[32,32,128]{2,1,0:T(8,128)(2,1)S(1)} async-done(((bf16[32,32,128]{2,1,0:T(8,128)(2,1)}), bf16[32,32,128]{2,1,0:T(8,128)(2,1)S(1)}, u32[]{:S(2)}, u32[]{:S(2)}) %all-to-all-start) | async-done | bytes 262176 | tf_op jit(solution)/shard_map/all_to_all | solution.py:331
  36.9 0.7 shard_map.106
  37.6 12.3 %all-to-all-start.1 = ((bf16[16,32,128]{2,1,0:T(8,128)(2,1)}), bf16[16,32,128]{2,1,0:T(8,128)(2,1)S(1)}, u32[]{:S(2)}, u32[]{:S(2)}) async-start(bf16[16,32,128]{2,1,0:T(8,128)(2,1)} %bitcast.4), calls=%async_computation.1 | async-start | bytes 262144 | tf_op jit(solution)/shard_map/all_to_all | solution.py:331
  50.0 0.7 collective-permute-start.4
  50.6 3.1 %collective-permute-start.5 = (bf16[96,128]{1,0:T(8,128)(2,1)S(1)}, bf16[96,128]{1,0:T(8,128)(2,1)S(1)}, u32[]{:S(2)}, u32[]{:S(2)}) collective-permute-start(bf16[96,128]{1,0:T(8,128)(2,1)S(1)} %get-tuple-element.35), channel_id=1, source_target_pairs={{1,2},{2,1},{5,6},{6,5},{9,10},{10,9},{13,14},{14,13},{17,18},{18,... | collective-permute-start | bytes 73736 | tf_op jit(solution)/shard_map/ppermute | solution.py:315
  53.8 0.0 collective-permute-done.4.refs_0_.refs_3_
  53.8 2.4 %collective-permute-done.5.refs_1_.refs_5_ = bf16[96,128]{1,0:T(8,128)(2,1)S(1)} collective-permute-done((bf16[96,128]{1,0:T(8,128)(2,1)S(1)}, bf16[96,128]{1,0:T(8,128)(2,1)S(1)}, u32[]{:S(2)}, u32[]{:S(2)}) %collective-permute-start.5) | collective-permute-done | bytes 24608 | tf_op jit(solution)/shard_map/ppermute | solution.py:315
  56.2 5.5 %all-to-all-done.1 = bf16[16,32,128]{2,1,0:T(8,128)(2,1)S(1)} async-done(((bf16[16,32,128]{2,1,0:T(8,128)(2,1)}), bf16[16,32,128]{2,1,0:T(8,128)(2,1)S(1)}, u32[]{:S(2)}, u32[]{:S(2)}) %all-to-all-start.1) | async-done | bytes 131104 | tf_op jit(solution)/shard_map/all_to_all | solution.py:331
  61.6 0.7 shard_map.107
  62.3 4.8 %all-to-all-start.2 = ((bf16[32,32,128]{2,1,0:T(8,128)(2,1)}), bf16[32,32,128]{2,1,0:T(8,128)(2,1)S(1)}, u32[]{:S(2)}, u32[]{:S(2)}) async-start(bf16[32,32,128]{2,1,0:T(8,128)(2,1)} %bitcast.6), calls=%async_computation.2 | async-start | bytes 524288 | tf_op jit(solution)/shard_map/all_to_all | solution.py:331
  67.1 3.3 %collective-permute-start.6 = (bf16[96,128]{1,0:T(8,128)(2,1)S(1)}, bf16[96,128]{1,0:T(8,128)(2,1)S(1)}, u32[]{:S(2)}, u32[]{:S(2)}) collective-permute-start(bf16[96,128]{1,0:T(8,128)(2,1)S(1)} %get-tuple-element.42), channel_id=1, source_target_pairs={{0,4},{4,0},{8,12},{12,8},{16,20},{20,16},{24,28},{28,24},{32,36},... | collective-permute-start | bytes 73736 | tf_op jit(solution)/shard_map/ppermute | solution.py:315
  70.4 2.5 %collective-permute-start.7 = (bf16[96,128]{1,0:T(8,128)(2,1)S(1)}, bf16[96,128]{1,0:T(8,128)(2,1)S(1)}, u32[]{:S(2)}, u32[]{:S(2)}) collective-permute-start(bf16[96,128]{1,0:T(8,128)(2,1)S(1)} %get-tuple-element.43), channel_id=1, source_target_pairs={{0,1},{1,0},{2,3},{3,2},{4,5},{5,4},{6,7},{7,6},{8,9},{9,8},{10,11... | collective-permute-start | bytes 73736 | tf_op jit(solution)/shard_map/ppermute | solution.py:315
  73.0 0.2 collective-permute-done.6.refs_4_
  73.2 0.6 collective-permute-done.7.refs_6_
  73.8 1.6 %all-to-all-done.2 = bf16[32,32,128]{2,1,0:T(8,128)(2,1)S(1)} async-done(((bf16[32,32,128]{2,1,0:T(8,128)(2,1)}), bf16[32,32,128]{2,1,0:T(8,128)(2,1)S(1)}, u32[]{:S(2)}, u32[]{:S(2)}) %all-to-all-start.2) | async-done | bytes 262176 | tf_op jit(solution)/shard_map/all_to_all | solution.py:331
  75.5 1.3 %shard_map.108 = (f32[7,96,192]{2,1,0:T(8,128)}, f32[1,192]{1,0:T(1,128)}, bf16[1,1,2,96,512]{4,3,2,1,0:T(8,128)(2,1)}) custom-call(bf16[1024,128]{1,0:T(8,128)(2,1)S(1)} %bitcast.11, f32[96,1024]{1,0:T(8,128)S(1)} %get-tuple-element.40.refs_1_, f32[16,128]{1,0:T(8,128)S(1)} %get-tuple-element.41.refs_2_, ...), custom_call_target="tpu_custom_call" | custom-call | tf_op jit(solution)/shard_map/pallas_call | solution.py:413
Async XLA Ops:
  0.6 16.7 %copy-start.1 = (bf16[1,1,2,96,512]{4,3,2,1,0:T(8,128)(2,1)S(1)}, bf16[1,1,2,96,512]{4,3,2,1,0:T(8,128)(2,1)}, u32[]{:S(2)}) copy-start(bf16[1,1,2,96,512]{4,3,2,1,0:T(8,128)(2,1)} %features_in.3) | copy-start | bytes 589828
  2.6 14.0 %collective-permute-start = (bf16[96,128]{1,0:T(8,128)(2,1)}, bf16[96,128]{1,0:T(8,128)(2,1)S(1)}, u32[]{:S(2)}, u32[]{:S(2)}) collective-permute-start(bf16[96,128]{1,0:T(8,128)(2,1)} %get-tuple-element.25), channel_id=1, source_target_pairs={{4,8},{8,4},{12,16},{16,12},{20,24},{24,20},{28,32},{32,28},{36,40... | collective-permute-start | bytes 73736 | tf_op jit(solution)/shard_map/ppermute | solution.py:308
  3.3 13.4 %collective-permute-start.1 = (bf16[96,128]{1,0:T(8,128)(2,1)}, bf16[96,128]{1,0:T(8,128)(2,1)S(1)}, u32[]{:S(2)}, u32[]{:S(2)}) collective-permute-start(bf16[96,128]{1,0:T(8,128)(2,1)} %get-tuple-element.26), channel_id=1, source_target_pairs={{0,4},{4,0},{8,12},{12,8},{16,20},{20,16},{24,28},{28,24},{32,36},... | collective-permute-start | bytes 73736 | tf_op jit(solution)/shard_map/ppermute | solution.py:308
  9.7 7.0 %collective-permute-start.2 = (bf16[96,128]{1,0:T(8,128)(2,1)}, bf16[96,128]{1,0:T(8,128)(2,1)S(1)}, u32[]{:S(2)}, u32[]{:S(2)}) collective-permute-start(bf16[96,128]{1,0:T(8,128)(2,1)} %get-tuple-element.27), channel_id=1, source_target_pairs={{1,2},{2,1},{5,6},{6,5},{9,10},{10,9},{13,14},{14,13},{17,18},{18,... | collective-permute-start | bytes 73736 | tf_op jit(solution)/shard_map/ppermute | solution.py:308
  14.0 3.3 %collective-permute-start.3 = (bf16[96,128]{1,0:T(8,128)(2,1)}, bf16[96,128]{1,0:T(8,128)(2,1)S(1)}, u32[]{:S(2)}, u32[]{:S(2)}) collective-permute-start(bf16[96,128]{1,0:T(8,128)(2,1)} %get-tuple-element.28), channel_id=1, source_target_pairs={{0,1},{1,0},{2,3},{3,2},{4,5},{5,4},{6,7},{7,6},{8,9},{9,8},{10,11... | collective-permute-start | bytes 73736 | tf_op jit(solution)/shard_map/ppermute | solution.py:308
  15.9 1.4 %copy-start.6 = (f32[192]{0:T(256)S(1)}, f32[192]{0:T(256)}, u32[]{:S(2)}) copy-start(f32[192]{0:T(256)} %param.11) | copy-start | bytes 2308
  17.3 0.7 copy-start.3
  21.3 7.3 %copy-start = (bf16[7,96,192]{2,1,0:T(8,128)(2,1)S(1)}, bf16[7,96,192]{2,1,0:T(8,128)(2,1)}, u32[]{:S(2)}) copy-start(bf16[7,96,192]{2,1,0:T(8,128)(2,1)} %param.10) | copy-start | bytes 774148
  21.3 7.3 %copy-start.5 = (s32[1,1,2,2]{3,2,1,0:T(2,128)S(1)}, s32[1,1,2,2]{3,2,1,0:T(2,128)}, u32[]{:S(2)}) copy-start(s32[1,1,2,2]{3,2,1,0:T(2,128)} %cross_in.3) | copy-start | bytes 52
  21.3 15.6 %all-to-all-start = ((bf16[32,32,128]{2,1,0:T(8,128)(2,1)}), bf16[32,32,128]{2,1,0:T(8,128)(2,1)S(1)}, u32[]{:S(2)}, u32[]{:S(2)}) async-start(bf16[32,32,128]{2,1,0:T(8,128)(2,1)} %bitcast.2), calls=%async_computation | async-start | bytes 524288 | tf_op jit(solution)/shard_map/all_to_all | solution.py:331
  28.6 0.7 copy-start.4
  29.3 1.0 %copy-start.2 = (bf16[256,1024]{1,0:T(8,128)(2,1)S(1)}, bf16[256,1024]{1,0:T(8,128)(2,1)}, u32[]{:S(2)}) copy-start(bf16[256,1024]{1,0:T(8,128)(2,1)} %get-tuple-element.30.grad) | copy-start | bytes 1572868
  37.6 24.0 %all-to-all-start.1 = ((bf16[16,32,128]{2,1,0:T(8,128)(2,1)}), bf16[16,32,128]{2,1,0:T(8,128)(2,1)S(1)}, u32[]{:S(2)}, u32[]{:S(2)}) async-start(bf16[16,32,128]{2,1,0:T(8,128)(2,1)} %bitcast.4), calls=%async_computation.1 | async-start | bytes 262144 | tf_op jit(solution)/shard_map/all_to_all | solution.py:331
  50.0 3.8 %collective-permute-start.4 = (bf16[96,128]{1,0:T(8,128)(2,1)S(1)}, bf16[96,128]{1,0:T(8,128)(2,1)S(1)}, u32[]{:S(2)}, u32[]{:S(2)}) collective-permute-start(bf16[96,128]{1,0:T(8,128)(2,1)S(1)} %get-tuple-element.34), channel_id=1, source_target_pairs={{4,8},{8,4},{12,16},{16,12},{20,24},{24,20},{28,32},{32,28},{36,40... | collective-permute-start | bytes 73736 | tf_op jit(solution)/shard_map/ppermute | solution.py:315
  50.6 5.5 %collective-permute-start.5 = (bf16[96,128]{1,0:T(8,128)(2,1)S(1)}, bf16[96,128]{1,0:T(8,128)(2,1)S(1)}, u32[]{:S(2)}, u32[]{:S(2)}) collective-permute-start(bf16[96,128]{1,0:T(8,128)(2,1)S(1)} %get-tuple-element.35), channel_id=1, source_target_pairs={{1,2},{2,1},{5,6},{6,5},{9,10},{10,9},{13,14},{14,13},{17,18},{18,... | collective-permute-start | bytes 73736 | tf_op jit(solution)/shard_map/ppermute | solution.py:315
  62.3 13.1 %all-to-all-start.2 = ((bf16[32,32,128]{2,1,0:T(8,128)(2,1)}), bf16[32,32,128]{2,1,0:T(8,128)(2,1)S(1)}, u32[]{:S(2)}, u32[]{:S(2)}) async-start(bf16[32,32,128]{2,1,0:T(8,128)(2,1)} %bitcast.6), calls=%async_computation.2 | async-start | bytes 524288 | tf_op jit(solution)/shard_map/all_to_all | solution.py:331
  67.1 6.1 %collective-permute-start.6 = (bf16[96,128]{1,0:T(8,128)(2,1)S(1)}, bf16[96,128]{1,0:T(8,128)(2,1)S(1)}, u32[]{:S(2)}, u32[]{:S(2)}) collective-permute-start(bf16[96,128]{1,0:T(8,128)(2,1)S(1)} %get-tuple-element.42), channel_id=1, source_target_pairs={{0,4},{4,0},{8,12},{12,8},{16,20},{20,16},{24,28},{28,24},{32,36},... | collective-permute-start | bytes 73736 | tf_op jit(solution)/shard_map/ppermute | solution.py:315
  70.4 3.4 %collective-permute-start.7 = (bf16[96,128]{1,0:T(8,128)(2,1)S(1)}, bf16[96,128]{1,0:T(8,128)(2,1)S(1)}, u32[]{:S(2)}, u32[]{:S(2)}) collective-permute-start(bf16[96,128]{1,0:T(8,128)(2,1)S(1)} %get-tuple-element.43), channel_id=1, source_target_pairs={{0,1},{1,0},{2,3},{3,2},{4,5},{5,4},{6,7},{7,6},{8,9},{9,8},{10,11... | collective-permute-start | bytes 73736 | tf_op jit(solution)/shard_map/ppermute | solution.py:315
